TPU v7x, 256 devices: a whole 4x4x8 slice. The times are simulated.
256 devices in a mesh: grp: 8 (over z), dp: 32 (over y, x, core).
Axes of the slice: x: 4, y: 4, z: 8, core: 2. Of those that a mesh axis runs over, the one named last changes fastest.
Arguments:
- attn: bfloat16 [131072, 2048], P(('grp', 'dp')), may hold values from -6 to 6
- hidden: bfloat16 [131072, 4096], P(('grp', 'dp')), may hold values from -6 to 6
- output_weight_rows: bfloat16 [2048, 4096], P('dp'), may hold values from -0.125 to 0.125
- down_factor: bfloat16 [2048, 16], replicated, may hold values from -0.125 to 0.125
- up_factor: bfloat16 [16, 4096], replicated, may hold values from -1.5 to 1.5
- final_norm_gain: float32 [4096], replicated, may hold values from 0.5 to 1.5
- queries: bfloat16 [512, 4096], P(('grp', 'dp')), may hold values from -6 to 6
- lengths: int32 [512], P(('grp', 'dp')), may hold values from 32 to 256
- offsets: int32 [512], P(('grp', 'dp')), may hold values from 0 to 256, as said below
- positives: int32 [512], P(('grp', 'dp')), may hold values from 0 to 511, as said below
Outputs:
- attention_gradient: bfloat16 [131072, 2048], P(('grp', 'dp'))
- query_gradient: float32 [512, 4096], P(('grp', 'dp'))
- down_factor_gradient: float32 [2048, 16], replicated
- up_factor_gradient: float32 [16, 4096], replicated
- loss: float32 [], replicated
Inputs may be any that keep to these rules, and one draw needn't show every extreme that they name: `offsets`: within each block of 2 passages the first offset is 0 and each next offset is the previous one plus the previous length rounded up to a multiple of 64; the last passage ends within the block's 512 rows. `positives`: each passage is the positive of exactly one query.
All inputs are finite; a program needn't handle non-finite values.
Results may differ from a plain program's by a relative error of at most 0.0077.
Values may be sent and summed in bfloat16 or wider, within the bound.
A program may use at most 128 MiB of HBM per device.

v0:
```python
import jax
import jax.numpy as jnp
from jax import lax
from jax.sharding import PartitionSpec as P


def per_device(
    attn,
    hidden,
    output_weight_rows,
    down_factor,
    up_factor,
    final_norm_gain,
    queries,
    lengths,
    offsets,
    positives,
):
    tok_rows = hidden.shape[0]
    pas_rows = lengths.shape[0]
    total = pas_rows * lax.axis_size("grp") * lax.axis_size("dp")
    values = hidden.astype(jnp.float32)
    rstd = lax.rsqrt(jnp.mean(values * values, axis=-1, keepdims=True) + 1e-05)
    normed = values * rstd
    shaped = normed * final_norm_gain
    rows = jnp.arange(tok_rows, dtype=jnp.int32)
    inside = (rows[None, :] >= offsets[:, None]) & (
        rows[None, :] < offsets[:, None] + lengths[:, None]
    )
    member = inside.astype(jnp.float32)
    counts = lengths.astype(jnp.float32)[:, None]
    pooled = jnp.dot(member, shaped, precision=lax.Precision.HIGHEST) / counts
    pnorm = jnp.sqrt(jnp.sum(pooled * pooled, axis=-1, keepdims=True) + 1e-06)
    embed = pooled / pnorm
    embed_b = embed.astype(jnp.bfloat16)
    query_f = queries.astype(jnp.float32)
    qnorm = jnp.sqrt(jnp.sum(query_f * query_f, axis=-1, keepdims=True) + 1e-06)
    unit = query_f / qnorm
    unit_b = unit.astype(jnp.bfloat16)
    columns = jnp.arange(total, dtype=jnp.int32)
    everyone = lax.all_gather(embed_b, ("grp", "dp"), axis=0, tiled=True)
    logits = 50.0 * jnp.dot(unit_b, everyone.T, preferred_element_type=jnp.float32)
    lse = jnp.log(jnp.sum(jnp.exp(logits), axis=-1))
    prob = jnp.exp(logits - lse[:, None])
    target = (positives[:, None] == columns[None, :]).astype(jnp.float32)
    loss_piece = jnp.sum(lse - jnp.sum(logits * target, axis=-1))
    grad_rows = ((prob - target) * 1024.0).astype(jnp.bfloat16)
    d_unit = 50.0 * jnp.dot(grad_rows, everyone, preferred_element_type=jnp.float32)
    d_embed = lax.psum_scatter(
        50.0 * jnp.dot(grad_rows.T, unit_b, preferred_element_type=jnp.float32),
        ("grp", "dp"),
        scatter_dimension=0,
        tiled=True,
    )
    query_gradient = (d_unit - unit * jnp.sum(unit * d_unit, axis=-1, keepdims=True)) / qnorm
    d_pooled = (d_embed - embed * jnp.sum(embed * d_embed, axis=-1, keepdims=True)) / pnorm
    dz = jnp.dot(member.T, d_pooled / counts, precision=lax.Precision.HIGHEST)
    dn = dz * final_norm_gain
    output_gradient = (rstd * (dn - normed * jnp.mean(dn * normed, axis=-1, keepdims=True))).astype(
        jnp.bfloat16
    )
    backward_lower = (
        2.0 * jnp.dot(output_gradient, up_factor.T, preferred_element_type=jnp.float32)
    ).astype(jnp.bfloat16)
    forward_lower = jnp.dot(attn, down_factor, preferred_element_type=jnp.float32).astype(
        jnp.bfloat16
    )
    frozen_product = jnp.dot(
        output_gradient,
        lax.all_gather(output_weight_rows, "dp", axis=0, tiled=True).T,
        preferred_element_type=jnp.float32,
    )
    attention_gradient = (
        frozen_product + jnp.dot(backward_lower, down_factor.T, preferred_element_type=jnp.float32)
    ).astype(jnp.bfloat16)
    down_factor_piece = jnp.dot(attn.T, backward_lower, preferred_element_type=jnp.float32)
    up_factor_piece = 2.0 * jnp.dot(
        forward_lower.T, output_gradient, preferred_element_type=jnp.float32
    )
    down_factor_gradient, up_factor_gradient, loss_running_sum = lax.psum(
        (down_factor_piece, up_factor_piece, loss_piece), ("grp", "dp")
    )
    loss = loss_running_sum / total
    return (attention_gradient, query_gradient, down_factor_gradient, up_factor_gradient, loss)


def solution(mesh):
    placed = (
        P(("grp", "dp"), None),
        P(("grp", "dp"), None),
        P("dp", None),
        P(),
        P(),
        P(),
        P(("grp", "dp"), None),
        P(("grp", "dp")),
        P(("grp", "dp")),
        P(("grp", "dp")),
    )
    return jax.shard_map(
        per_device,
        mesh=mesh,
        in_specs=placed,
        out_specs=(P(("grp", "dp"), None), P(("grp", "dp"), None), P(), P(), P()),
        check_vma=False,
    )
```

profile of v0, /device:TPU:1, one launch (start us, length us, event | category | flops | bytes accessed | tf_op | source)
XLA Modules:
  0.0 726.3 jit_solution(7556966569824507074)
XLA Ops:
  8.0 0.0 all-gather.6.cloned.1.call-start
  8.1 3.2 fusion.9
  11.4 0.3 copy-done.2
  11.6 4.4 fusion.18
  16.1 0.7 convert_bitcast_fusion
  16.8 0.0 all-reduce.5.cloned.1.call-start
  16.9 0.1 fusion.15
  17.0 119.3 %all-gather.6.cloned.1.call-done = bf16[256,2,4096]{2,1,0:T(2,128)(2,1)} async-done(((bf16[1,2,4096]{2,1,0:T(2,128)(2,1)}), bf16[256,2,4096]{2,1,0:T(2,128)(2,1)}) %all-gather.6.cloned.1.call-update) | async-done | bytes 4194320 | tf_op jit(solution)/shard_map/all_gather | solution.py:41
  136.3 7.2 reshape.46
  143.5 3.5 select_reduce_fusion
  147.0 0.6 subtract_reduce_fusion
  147.7 4.6 convolution_multiply_fusion
  152.3 0.0 all-gather.4.cloned.1.call-start
  152.3 0.5 all-gather.4.cloned.1.call-update
  152.9 0.0 all-reduce.7.cloned.1.call-start
  152.9 76.2 %psum.23 = f32[]{:T(128)} all-reduce(f32[]{:T(128)} %get-tuple-element.11), channel_id=1, replica_groups=mesh['grp'=8,'dp'=32] {'grp','dp'}, use_global_device_ids=true, to_apply=%region_12.0 | all-reduce | flops 1 | bytes 8 | tf_op jit(solution)/shard_map/psum | solution.py:80
  229.8 3.2 multiply_reduce_fusion
  232.9 0.7 subtract_divide_fusion
  233.6 209.1 %all-reduce.5.cloned.1.call-done = f32[512,4096]{1,0:T(8,128)} async-done(((f32[512,4096]{1,0:T(8,128)}), f32[512,4096]{1,0:T(8,128)}) %all-reduce.5.cloned.1.call-update) | async-done | bytes 8388624
  442.7 1.1 multiply_reduce_fusion.1
  443.8 7.4 %fusion.5 = (f32[512]{0:T(512)S(1)}, f32[512,4096]{1,0:T(8,128)S(1)}) fusion(bf16[512,4096]{1,0:T(8,128)(2,1)} %param.11, f32[4096]{0:T(1024)S(1)} %copy-done.8, f32[512]{0:T(512)S(1)} %add_rsqrt_fusion, f32[2,4096]{1,0:T(2,128)S(1)} %get-tuple-element.10, f32[512,4096]{1,0:T(8,128)} %all-reduce.5.cloned.1.call-done, u32[]{:T(128)S(6)} %multiply.21, ...), kind=kOutput, calls=%fused_computation.6 | convolution fusion | flops 60844544 | bytes 12668964 | tf_op jit(solution)/shard_map/dot_general | solution.py:57
  451.3 2.8 fusion.8
  454.1 2.0 copy-done.4
  456.0 1.2 fusion.12
  457.2 1.1 convolution_bitcast_fusion
  458.3 2.7 fusion.26
  461.0 5.2 convolution_multiply_fusion.1
  466.2 0.0 all-gather.4.cloned.1.call-done
  466.2 15.6 %add_convert_fusion = bf16[512,2048]{1,0:T(8,128)(2,1)} fusion(f32[512,2048]{1,0:T(8,128)} %fusion.26, bf16[512,4096]{1,0:T(8,128)(2,1)} %copy-done.4, bf16[2048,4096]{1,0:T(8,128)(2,1)} %all-gather.4.cloned.1.call-done), kind=kOutput, calls=%fused_computation.14 | convolution fusion | flops 8592031744 | bytes 27262976 | tf_op jit(solution)/shard_map/dot_general | solution.py:68
  481.8 233.0 %all-reduce.7.cloned.1.call-done = (f32[2048,16]{0,1:T(8,128)}, f32[16,4096]{1,0:T(8,128)}) async-done(((f32[2048,16]{0,1:T(8,128)}, f32[16,4096]{1,0:T(8,128)}), (f32[2048,16]{0,1:T(8,128)}, f32[16,4096]{1,0:T(8,128)})) %all-reduce.7.cloned.1.call-update) | async-done | bytes 393232 | tf_op jit(solution)/shard_map/psum | solution.py:80
  714.8 1.6 copy.18
  716.4 1.7 copy.19
  (30 shorter events, 0.1 us)
Async XLA Ops:
  8.0 449.2 %copy-start = (bf16[512,2048]{1,0:T(8,128)(2,1)S(1)}, bf16[512,2048]{1,0:T(8,128)(2,1)}, u32[]{:S(2)}) copy-start(bf16[512,2048]{1,0:T(8,128)(2,1)} %param.10) | copy-start | bytes 6291460
  8.0 3.3 copy-start.11
  8.0 3.3 copy-start.10
  8.0 128.3 %all-gather.6.cloned.1.call-start = ((), (), s32[]{:S(2)}) async-start(), calls=%async_computation.1 | async-start | bytes 4210688 | tf_op jit(solution)/shard_map/all_gather | solution.py:41
  8.1 3.6 copy-start.2
  11.3 5.5 copy-start.5
  16.8 425.9 %all-reduce.5.cloned.1.call-start = ((), (), s32[]{:S(2)}) async-start(), calls=%async_computation.2 | async-start | bytes 16777216
  17.0 126.5 %copy-start.9 = (s32[2]{0:T(128)S(1)}, s32[2]{0:T(128)}, u32[]{:S(2)}) copy-start(s32[2]{0:T(128)} %param.19) | copy-start | bytes 28
  152.3 291.5 %copy-start.8 = (f32[4096]{0:T(1024)S(1)}, f32[4096]{0:T(1024)}, u32[]{:S(2)}) copy-start(f32[4096]{0:T(1024)} %param.15) | copy-start | bytes 49156
  152.3 313.9 %all-gather.4.cloned.1.call-start = ((), (), s32[]{:S(2)}) async-start(), calls=%async_computation | async-start | bytes 17301504 | tf_op jit(solution)/shard_map/all_gather | solution.py:70
  152.9 561.9 %all-reduce.7.cloned.1.call-start = ((), (), s32[]{:S(2)}) async-start(), calls=%async_computation.3 | async-start | bytes 786432 | tf_op jit(solution)/shard_map/psum | solution.py:80
  443.8 7.4 %copy-start.3 = (bf16[512,4096]{1,0:T(8,128)(2,1)S(1)}, bf16[512,4096]{1,0:T(8,128)(2,1)}, u32[]{:S(2)}) copy-start(bf16[512,4096]{1,0:T(8,128)(2,1)} %param.11) | copy-start | bytes 12582916
  451.2 4.8 copy-start.7
  454.1 2.0 copy-start.4
  456.0 2.3 copy-start.6
  466.2 251.8 %copy-start.1 = (bf16[512,2048]{1,0:T(8,128)(2,1)S(1)}, bf16[512,2048]{1,0:T(8,128)(2,1)}, u32[]{:S(2)}) copy-start(bf16[512,2048]{1,0:T(8,128)(2,1)} %param.10) | copy-start | bytes 6291460
Sparse Core Ops, SparseCore 0:
  16.9 119.3 all-gather.5
  152.4 290.2 all-reduce.4
  466.3 248.4 all-reduce.6
Sparse Core Ops, SparseCore 1:
  155.6 78.8 all-gather.3
where the time goes:
time: 727 us; the launch traced here: 726 us
  waiting for transfers between devices  562 us (77%)
  blocking collectives  76.2 us (10%)
  matrix products  48.8 us (7%)
  between operations  17.2 us (2%)
  local copies, waits for them, and re-layouts  12.7 us (2%)
  other arithmetic  9.32 us (1%)
    psum x1, waiting for transfers between devices, per_device(): lax.psum((down_factor_piece, up_factor_piece, loss_piece), ('grp', 'dp'))  233 us
    unnamed x5, waiting for transfers between devices  210 us
    all_gather x1, waiting for transfers between devices, per_device(): everyone = lax.all_gather(embed_b, ('grp', 'dp'), axis=0, tiled=True)  119 us
    psum x1, blocking collectives, per_device(): lax.psum((down_factor_piece, up_factor_piece, loss_piece), ('grp', 'dp'))  76.2 us
    dot_general x1, matrix products, per_device(): jnp.dot(output_gradient, lax.all_gather(output_weight_rows, 'dp', axis=0,...  15.6 us
  transfers between devices with their start and end apart: 4, of which 3 were waited for; matrix products, arithmetic and copies ran while one was open for 6% of the time, Pallas kernels for 0%

commit v1 on v0

v1 whole, which is shorter than its diff:
```python
import functools

import jax
import jax.numpy as jnp
from jax import lax
from jax.experimental import pallas as pl
from jax.experimental.pallas import tpu as pltpu
from jax.sharding import PartitionSpec as P

MESH = pl.DeviceIdType.MESH
F32 = jnp.float32
BF16 = jnp.bfloat16
HI = lax.Precision.HIGHEST
NT = (((1,), (1,)), ((), ()))
TN = (((0,), (0,)), ((), ()))


def iota(shape, dim):
    return lax.broadcasted_iota(jnp.int32, shape, dim)


def mm(a, b, dims=None, precision=None):
    if dims is None:
        dims = (((1,), (0,)), ((), ()))
    return lax.dot_general(a, b, dims, precision=precision, preferred_element_type=F32)


def split3(x):
    high = x.astype(BF16).astype(F32)
    rest = x - high
    mid = rest.astype(BF16).astype(F32)
    return high, mid, (rest - mid).astype(BF16).astype(F32)


def kernel(
    ng,
    nq,
    hidden,
    attn,
    down_t,
    up,
    gain,
    queries,
    lengths,
    offsets,
    positives,
    dy_out,
    blt_out,
    query_out,
    adapter_out,
    loss_out,
    hv,
    av,
    dyv,
    ub,
    eb,
    unit_s,
    pool_s,
    ssq_s,
    col_s,
    dn_s,
    lx,
    dpb,
    rb,
    dub,
    rub,
    ab,
    core_in,
    plane_in,
    z_in,
    total_s,
    local_sem,
    u_send,
    u_recv,
    e_send,
    e_recv,
    x_send,
    x_recv,
    d_send,
    d_recv,
    v_send,
    v_recv,
    c_send,
    c_recv,
    p_send,
    p_recv,
    z_send,
    z_recv,
    g_send,
    g_recv,
    s_send,
    s_recv,
):
    nl = 2 * ng
    tok, width = hv.shape
    wc = width // 8
    feat = av.shape[1]
    passages = 2 * nl * nq
    grp = lax.axis_index("grp")
    dp = lax.axis_index("dp")
    core = lax.rem(dp, 2)
    q_me = lax.div(dp, 2)
    l_me = 2 * grp + core

    def plane_peer(o):
        q = lax.rem(q_me + o, nq)
        return q, (grp, 2 * q + core)

    def line_peer(o):
        l = lax.rem(l_me + o, nl)
        return l, (lax.div(l, 2), 2 * q_me + lax.rem(l, 2))

    def z_peer(o):
        z = lax.rem(grp + o, ng)
        return z, (z, dp)

    def fan_out(n, peer, source, target, me, send, recv):
        def body(o, carry):
            there, device = peer(o)
            pltpu.make_async_remote_copy(
                src_ref=source(there),
                dst_ref=target.at[me],
                send_sem=send.at[there],
                recv_sem=recv.at[me],
                device_id=device,
                device_id_type=MESH,
            ).start()
            return carry

        lax.fori_loop(1, n, body, 0)

    def fan_wait(n, peer, target, me, recv):
        def body(o, carry):
            there, device = peer(o)
            pltpu.make_async_remote_copy(
                src_ref=target.at[there],
                dst_ref=target.at[there],
                send_sem=recv.at[there],
                recv_sem=recv.at[there],
                device_id=device,
                device_id_type=MESH,
            ).wait_recv()
            return carry

        lax.fori_loop(1, n, body, 0)

    def fan_drain(n, peer, source, send):
        def body(o, carry):
            there, device = peer(o)
            pltpu.make_async_remote_copy(
                src_ref=source(there),
                dst_ref=source(there),
                send_sem=send.at[there],
                recv_sem=send.at[there],
                device_id=device,
                device_id_type=MESH,
            ).wait_send()
            return carry

        lax.fori_loop(1, n, body, 0)

    load_hidden = pltpu.make_async_copy(hidden, hv, local_sem.at[0])
    load_attn = pltpu.make_async_copy(attn, av, local_sem.at[1])
    load_hidden.start()
    load_attn.start()

    barrier = pltpu.get_barrier_semaphore()

    def greet(n, peer):
        def body(o, carry):
            _, device = peer(o)
            pl.semaphore_signal(barrier, inc=1, device_id=device, device_id_type=MESH)
            return carry

        lax.fori_loop(1, n, body, 0)

    greet(nq, plane_peer)
    greet(nl, line_peer)

    odd16 = lax.rem(iota((16, 1), 0), 2) == 1

    def by_row(even, odd):
        return jnp.where(odd16, odd, even)

    def pair_sum(x):
        even = jnp.sum(jnp.where(odd16, 0.0, x), axis=0, keepdims=True)
        odd = jnp.sum(jnp.where(odd16, x, 0.0), axis=0, keepdims=True)
        return by_row(even, odd)

    def chunk(k):
        return slice(k * wc, (k + 1) * wc)

    for k in range(8):
        unit_s[2 * k : 2 * k + 2, :] = queries[:, chunk(k)].astype(F32)
    query16 = unit_s[...]
    qnorm = jnp.sqrt(pair_sum(jnp.sum(query16 * query16, axis=1, keepdims=True)) + 1e-06)
    unit16 = query16 / qnorm
    unit_s[...] = unit16
    ub[l_me, :, 0:wc] = unit16.astype(BF16)
    place = jnp.broadcast_to(by_row(positives[0], positives[1]), (16, 128))
    lane16 = iota((16, 128), 1)
    high_place = lax.shift_right_logical(place, 4)
    digits = jnp.where(lane16 == 0, high_place, jnp.where(lane16 == 1, place - 16 * high_place, 0))
    ub[l_me, :, wc:] = digits.astype(F32).astype(BF16)

    pl.semaphore_wait(barrier, nq - 1 + nl - 1)
    fan_out(nl, line_peer, lambda there: ub.at[l_me], ub, l_me, u_send, u_recv)

    load_hidden.wait()

    def squares(i, carry):
        rows = pl.ds(pl.multiple_of(i * 16, 16), 16)
        v = hv[rows, :].astype(F32)
        ssq_s[rows, :] = jnp.broadcast_to(jnp.sum(v * v, axis=1, keepdims=True), (16, 128))
        return carry

    lax.fori_loop(0, tok // 16, squares, 0)
    ssq_row = jnp.transpose(ssq_s[...])[0:1, :]
    rstd = lax.rsqrt(ssq_row * (1.0 / width) + 1e-05)
    token = iota((1, tok), 1)
    inside0 = (token >= offsets[0]) & (token < offsets[0] + lengths[0])
    inside1 = (token >= offsets[1]) & (token < offsets[1] + lengths[1])
    w0 = jnp.where(inside0, rstd, 0.0)
    w1 = jnp.where(inside1, rstd, 0.0)
    counts = by_row(lengths[0].astype(F32), lengths[1].astype(F32))
    row16 = iota((16, 1), 0)
    wh, wm, wl = split3(jnp.where(odd16, w1, w0))
    part = lax.div(row16, 2)
    w3 = jnp.where(part == 0, wh, jnp.where(part == 1, wm, jnp.where(part == 2, wl, 0.0))).astype(BF16)
    for k in range(8):
        p = mm(w3, hv[:, chunk(k)])
        pool_s[2 * k : 2 * k + 2, :] = (p[0:2] + p[2:4] + p[4:6]) * gain[0:1, chunk(k)]
    pooled = pool_s[...] / counts
    pnorm = jnp.sqrt(pair_sum(jnp.sum(pooled * pooled, axis=1, keepdims=True)) + 1e-06)
    embed = pooled / pnorm
    eb[q_me] = embed.astype(BF16)
    fan_out(nq, plane_peer, lambda there: eb.at[q_me], eb, q_me, e_send, e_recv)

    load_attn.wait()
    flt = mm(down_t[...], av[...], NT).astype(BF16)
    hut = mm(up[...], hv[...], NT)
    na, nb = 16 * nq, 16 * nl
    np_, nqr = 2 * nq, 2 * nl

    def spread(rows, cols, row_is_block):
        small = iota((rows, cols), 0 if row_is_block else 1)
        big = iota((rows, cols), 1 if row_is_block else 0)
        return small == 2 * lax.div(big, 16) + lax.rem(big, 2)

    def as_f32(m):
        return jnp.where(m, 1.0, 0.0)

    same_chunk = lax.div(lax.rem(iota((na, nb), 0), 16), 2) == lax.div(lax.rem(iota((na, nb), 1), 16), 2)
    gather_a = as_f32(spread(np_, na, True))
    gather_b = as_f32(spread(nb, 128, False))
    first_b = as_f32(spread(nb, 128, False) & (lax.rem(iota((nb, 128), 0), 16) < 2))
    scatter_a = as_f32(spread(na, np_, False)).astype(BF16)
    scatter_b = as_f32(spread(128, nb, True)).astype(BF16)

    fan_wait(nl, line_peer, ub, l_me, u_recv)
    ubm = ub[:, :, 0:wc].reshape(nb, wc)
    digit = as_f32(iota((16, 128), 0) == iota((16, 128), 1)).astype(BF16)
    place_b = mm(digit, ub[:, :, wc:].reshape(nb, 128), NT).astype(BF16)
    place_i = mm(place_b, first_b.astype(BF16))
    pos = 16.0 * place_i[0:1, :] + place_i[1:2, :]
    passage = iota((np_, 1), 0)
    number = 2 * (grp * 2 * nq + 2 * lax.div(passage, 2) + core) + lax.rem(passage, 2)
    used = iota((1, 128), 1) < nqr
    target = jnp.where((number.astype(F32) == pos) & used, 1.0, 0.0)

    fan_wait(nq, plane_peer, eb, q_me, e_recv)
    ebm = eb[...].reshape(na, wc)
    products = jnp.where(same_chunk, mm(ebm, ubm, NT), 0.0)
    logits = 50.0 * mm(mm(gather_a, products, precision=HI), gather_b, precision=HI)
    expo = jnp.where(used, jnp.exp(logits), 0.0)
    partial = jnp.sum(expo, axis=0, keepdims=True)
    chosen = jnp.sum(logits * target, axis=0, keepdims=True)
    row8 = iota((8, 128), 0)
    lx[l_me] = jnp.where(row8 == 0, partial, jnp.where(row8 == 1, chosen, 0.0))
    fan_out(nl, line_peer, lambda there: lx.at[l_me], lx, l_me, x_send, x_recv)
    fan_wait(nl, line_peer, lx, l_me, x_recv)
    line = jnp.sum(lx[...], axis=0)
    lse = jnp.log(jnp.where(used, line[0:1, :], 1.0))
    line_loss = jnp.sum(jnp.where(used, lse - line[1:2, :], 0.0), axis=1, keepdims=True)
    prob = jnp.exp(logits - lse)
    grad = jnp.where(used, (prob - target) * 1024.0, 0.0).astype(BF16)
    spread_grad = mm(mm(scatter_a, grad).astype(BF16), scatter_b)
    g1 = jnp.where(same_chunk, spread_grad, 0.0)
    dpb[:, :, 0:wc] = mm(g1.astype(BF16), ubm).reshape(nq, 16, wc)
    dpb[:, :, wc:] = jnp.broadcast_to(jnp.where(iota((1, 1, 128), 2) == q_me, line_loss.reshape(1, 1, 1), 0.0), (nq, 16, 128))
    rb[q_me] = dpb[q_me]
    fan_out(nq, plane_peer, lambda there: dpb.at[there], rb, q_me, d_send, d_recv)
    dub[...] = mm(jnp.transpose(g1).astype(BF16), ebm).reshape(nl, 16, wc)
    rub[l_me] = dub[l_me]
    fan_out(nl, line_peer, lambda there: dub.at[there], rub, l_me, v_send, v_recv)

    fan_wait(nq, plane_peer, rb, q_me, d_recv)
    gathered = jnp.sum(rb[...], axis=0)
    loss_out[...] = jnp.broadcast_to(
        jnp.sum(gathered[0:8, wc:], axis=1, keepdims=True) * (1.0 / passages), (8, 128)
    )
    d_embed = 50.0 * gathered[:, 0:wc]
    along = pair_sum(jnp.sum(embed * d_embed, axis=1, keepdims=True))
    pool_s[...] = (d_embed - embed * along) / pnorm / counts
    dn_s[...] = jnp.zeros_like(dn_s)
    for k in range(8):
        dn = pool_s[2 * k : 2 * k + 2, :] * gain[0:1, chunk(k)]
        dh, dm, dl = split3(dn)
        dn_s[0:2, chunk(k)] = dh
        dn_s[2:4, chunk(k)] = dm
        dn_s[4:6, chunk(k)] = dl
        dn_s[8:10, chunk(k)] = dn
    dn3 = jnp.where(row16 < 6, dn_s[...], 0.0).astype(BF16)

    s3 = mm(dn3, hv[...], NT)
    s0 = s3[0:1] + s3[2:3] + s3[4:5]
    s1 = s3[1:2] + s3[3:4] + s3[5:6]
    s = jnp.where(inside0, s0, jnp.where(inside1, s1, 0.0))
    b = rstd * rstd * rstd * s * (1.0 / width)
    u3 = mm(up[...], dn3, NT)
    u0 = u3[:, 0:1] + u3[:, 2:3] + u3[:, 4:5]
    u1 = u3[:, 1:2] + u3[:, 3:4] + u3[:, 5:6]
    blt = (2.0 * (u0 * w0 + u1 * w1 - b * hut)).astype(BF16)
    blt_out[...] = blt
    tiles_down, tiles_up = feat // 128, width // 128
    per = (tiles_down + tiles_up) // nq

    def put(t, x):
        ab[t // per, :, (t % per) * 128 : (t % per) * 128 + 128] = x

    def get(ref, t):
        return ref[t // per, :, (t % per) * 128 : (t % per) * 128 + 128]

    down_part = mm(blt, av[...])
    for t in range(tiles_down):
        put(t, down_part[:, t * 128 : t * 128 + 128])
    fl = flt.astype(F32)
    fb = b * fl
    fbh = fb.astype(BF16)
    fbl = (fb - fbh.astype(F32)).astype(BF16)
    f0 = jnp.sum(w0 * fl, axis=1, keepdims=True)
    f1 = jnp.sum(w1 * fl, axis=1, keepdims=True)
    for k in range(8):
        hk = hv[:, chunk(k)]
        up2 = mm(fbh, hk) + mm(fbl, hk)
        up_part = 2.0 * (f0 * dn_s[8:9, chunk(k)] + f1 * dn_s[9:10, chunk(k)] - up2)
        for t in range(wc // 128):
            put(tiles_down + k * (wc // 128) + t, up_part[:, t * 128 : t * 128 + 128])

    def half(which):
        return pl.ds(pl.multiple_of(8 * which, 8), 8)

    other = 1 - core
    swap = pltpu.make_async_remote_copy(
        src_ref=ab.at[:, half(other), :],
        dst_ref=core_in,
        send_sem=c_send,
        recv_sem=c_recv,
        device_id=(grp, 2 * q_me + other),
        device_id_type=MESH,
    )
    swap.start()

    cols = jnp.where(
        iota((128, tok), 0) == 0, w0, jnp.where(iota((128, tok), 0) == 1, w1, b)
    )
    col_s[...] = jnp.transpose(cols)
    swap.wait()
    mine = half(core)
    core_in[...] = core_in[...] + ab[:, mine, :]
    plane_in[q_me] = core_in[q_me]
    fan_out(nq, plane_peer, lambda there: core_in.at[there], plane_in, q_me, p_send, p_recv)

    def rows_dy(i, carry):
        rows = pl.ds(pl.multiple_of(i * 16, 16), 16)
        c = col_s[rows, :]
        v = hv[rows, :].astype(F32)
        dyv[rows, :] = (c[:, 0:1] * dn_s[8:9, :] + c[:, 1:2] * dn_s[9:10, :] - c[:, 2:3] * v).astype(BF16)
        return carry

    lax.fori_loop(0, tok // 16, rows_dy, 0)
    store_dy = pltpu.make_async_copy(dyv, dy_out, local_sem.at[2])
    store_dy.start()

    fan_wait(nq, plane_peer, plane_in, q_me, p_recv)
    z_in[grp] = jnp.sum(plane_in[...], axis=0)
    fan_out(ng, z_peer, lambda there: z_in.at[grp], z_in, grp, z_send, z_recv)

    fan_wait(nl, line_peer, rub, l_me, v_recv)
    d_unit = 50.0 * jnp.sum(rub[...], axis=0)
    unit = unit_s[...]
    unit_s[...] = (d_unit - unit * pair_sum(jnp.sum(unit * d_unit, axis=1, keepdims=True))) / qnorm
    for k in range(8):
        query_out[:, chunk(k)] = unit_s[2 * k : 2 * k + 2, :]

    fan_wait(ng, z_peer, z_in, grp, z_recv)
    total_s[q_me, mine, :] = jnp.sum(z_in[...], axis=0)

    def gather_piece(o, carry):
        there, device = plane_peer(o)
        pltpu.make_async_remote_copy(
            src_ref=total_s.at[q_me, mine, :],
            dst_ref=total_s.at[q_me, mine, :],
            send_sem=g_send.at[there],
            recv_sem=g_recv.at[q_me],
            device_id=device,
            device_id_type=MESH,
        ).start()
        return carry

    def gather_wait(o, carry):
        there, device = plane_peer(o)
        piece = total_s.at[there, mine, :]
        pltpu.make_async_remote_copy(
            src_ref=piece,
            dst_ref=piece,
            send_sem=g_send.at[there],
            recv_sem=g_recv.at[there],
            device_id=device,
            device_id_type=MESH,
        ).wait()
        return carry

    lax.fori_loop(1, nq, gather_piece, 0)
    lax.fori_loop(1, nq, gather_wait, 0)
    back = pltpu.make_async_remote_copy(
        src_ref=total_s.at[:, mine, :],
        dst_ref=total_s.at[:, mine, :],
        send_sem=s_send,
        recv_sem=s_recv,
        device_id=(grp, 2 * q_me + other),
        device_id_type=MESH,
    )
    back.start()
    fan_drain(nl, line_peer, lambda there: ub.at[there], u_send)
    fan_drain(nq, plane_peer, lambda there: eb.at[there], e_send)
    fan_drain(nl, line_peer, lambda there: lx.at[there], x_send)
    fan_drain(nq, plane_peer, lambda there: dpb.at[there], d_send)
    fan_drain(nl, line_peer, lambda there: dub.at[there], v_send)
    fan_drain(nq, plane_peer, lambda there: core_in.at[there], p_send)
    fan_drain(ng, z_peer, lambda there: z_in.at[there], z_send)
    store_dy.wait()
    back.wait()
    for t in range(tiles_down + tiles_up):
        adapter_out[:, t * 128 : t * 128 + 128] = get(total_s, t)


def per_device(ng, nq, attn, hidden, weight, down, up, gain, queries, lengths, offsets, positives):
    tok, width = hidden.shape
    feat = attn.shape[1]
    wc = width // 8
    nl = 2 * ng
    piece = (feat + width) // nq
    down_t = down.T
    vmem = pl.BlockSpec(memory_space=pltpu.VMEM)
    smem = pl.BlockSpec(memory_space=pltpu.SMEM)
    anywhere = pl.BlockSpec(memory_space=pl.ANY)
    dma = pltpu.SemaphoreType.DMA
    everything = lax.all_gather(weight, "dp", axis=0, tiled=True)
    dy, blt, query_gradient, adapters, loss = pl.pallas_call(
        functools.partial(kernel, ng, nq),
        out_shape=(
            jax.ShapeDtypeStruct((tok, width), BF16),
            jax.ShapeDtypeStruct((16, tok), BF16),
            jax.ShapeDtypeStruct((2, width), F32),
            jax.ShapeDtypeStruct((16, feat + width), F32),
            jax.ShapeDtypeStruct((8, 128), F32),
        ),
        in_specs=[anywhere, anywhere, vmem, vmem, vmem, vmem, smem, smem, smem],
        out_specs=(anywhere, vmem, vmem, vmem, vmem),
        scratch_shapes=[
            pltpu.VMEM((tok, width), BF16),
            pltpu.VMEM((tok, feat), BF16),
            pltpu.VMEM((tok, width), BF16),
            pltpu.VMEM((nl, 16, wc + 128), BF16),
            pltpu.VMEM((nq, 16, wc), BF16),
            pltpu.VMEM((16, wc), F32),
            pltpu.VMEM((16, wc), F32),
            pltpu.VMEM((tok, 128), F32),
            pltpu.VMEM((tok, 128), F32),
            pltpu.VMEM((16, width), F32),
            pltpu.VMEM((nl, 8, 128), F32),
            pltpu.VMEM((nq, 16, wc + 128), F32),
            pltpu.VMEM((nq, 16, wc + 128), F32),
            pltpu.VMEM((nl, 16, wc), F32),
            pltpu.VMEM((nl, 16, wc), F32),
            pltpu.VMEM((nq, 16, piece), F32),
            pltpu.VMEM((nq, 8, piece), F32),
            pltpu.VMEM((nq, 8, piece), F32),
            pltpu.VMEM((ng, 8, piece), F32),
            pltpu.VMEM((nq, 16, piece), F32),
            dma((3,)),
            dma((nl,)),
            dma((nl,)),
            dma((nq,)),
            dma((nq,)),
            dma((nl,)),
            dma((nl,)),
            dma((nq,)),
            dma((nq,)),
            dma((nl,)),
            dma((nl,)),
            dma,
            dma,
            dma((nq,)),
            dma((nq,)),
            dma((ng,)),
            dma((ng,)),
            dma((nq,)),
            dma((nq,)),
            dma,
            dma,
        ],
        compiler_params=pltpu.CompilerParams(
            collective_id=0, has_side_effects=True, vmem_limit_bytes=40 * 1024 * 1024
        ),
    )(hidden, attn, down_t, up, gain.reshape(1, width), queries, lengths, offsets, positives)
    attention_gradient = (
        mm(dy, everything, NT) + mm(blt, down_t, TN)
    ).astype(BF16)
    return (
        attention_gradient,
        query_gradient,
        adapters[:, 0:feat].T,
        adapters[:, feat:],
        loss[0, 0],
    )


def solution(mesh):
    ng = mesh.shape["grp"]
    nq = mesh.shape["dp"] // 2
    both = P(("grp", "dp"))
    rows = P(("grp", "dp"), None)
    return jax.shard_map(
        functools.partial(per_device, ng, nq),
        mesh=mesh,
        in_specs=(rows, rows, P("dp", None), P(), P(), P(), rows, both, both, both),
        out_specs=(rows, rows, P(), P(), P()),
        check_vma=False,
    )
```

time: 727 us -> 122 us (0.17)
  waiting for transfers between devices: 562 us -> 8.57 us
  blocking collectives: 76.2 us -> 0 us
  Pallas kernels: 0 us -> 69.2 us
  matrix products: 48.8 us -> 17.9 us
  other arithmetic: 9.32 us -> 0 us
    psum x1 -> x0, waiting for transfers between devices: 233 us -> none  [per_device(): lax.psum((down_factor_piece, up_factor_piece, loss_piece), ('grp', 'dp'))]
    unnamed x5 -> x1, waiting for transfers between devices: 210 us -> 0.68 us
    all_gather x2 -> x1, waiting for transfers between devices: 119 us -> 7.89 us  [per_device(): everything = lax.all_gather(weight, 'dp', axis=0, tiled=True)]
    psum x1 -> x0, blocking collectives: 76.2 us -> none  [per_device(): lax.psum((down_factor_piece, up_factor_piece, loss_piece), ('grp', 'dp'))]
    pallas_call x0 -> x1, Pallas kernels: none -> 69.2 us  [per_device(): pl.pallas_call(functools.partial(kernel, ng, nq), out_shape=(jax.ShapeDty...]
    dot_general x10 -> x2, matrix products: 48.8 us -> 17.9 us  [mm(): lax.dot_general(a, b, dims, precision=precision, preferred_element_type=F32)]
  transfers between devices with their start and end apart: 4 -> 1, of which waited for: 3 -> 1; matrix products, arithmetic and copies ran while one was open for 6% -> 4% of each run, Pallas kernels for 0% -> 57%
where the time goes in v1:
time: 122 us
  Pallas kernels  69.2 us (57%)
  matrix products  17.9 us (15%)
  between operations  14.1 us (12%)
  local copies, waits for them, and re-layouts  11.9 us (10%)
  waiting for transfers between devices  8.57 us (7%)
    pallas_call x1, Pallas kernels, per_device(): pl.pallas_call(functools.partial(kernel, ng, nq), out_shape=(jax.ShapeDty...  69.2 us
    dot_general x2, matrix products, mm(): lax.dot_general(a, b, dims, precision=precision, preferred_element_type=F32)  17.9 us
    unnamed x21, local copies, waits for them, and re-layouts  9.53 us
    all_gather x1, waiting for transfers between devices, per_device(): everything = lax.all_gather(weight, 'dp', axis=0, tiled=True)  7.89 us
  transfers between devices with their start and end apart: 1, of which 1 were waited for; matrix products, arithmetic and copies ran while one was open for 4% of the time, Pallas kernels for 57%

profile of v1, /device:TPU:1, one launch (start us, length us, event | category | flops | bytes accessed | tf_op | source)
XLA Modules:
  0.0 121.6 jit_solution(10330390395066161818)
XLA Ops:
  7.2 0.0 all-gather.2.cloned.1.call-start
  7.2 0.7 all-gather.2.cloned.1.call-update
  7.9 0.0 copy-start
  7.9 2.2 %copy-done = bf16[512,4096]{1,0:T(8,128)(2,1)S(1)} copy-done((bf16[512,4096]{1,0:T(8,128)(2,1)S(1)}, bf16[512,4096]{1,0:T(8,128)(2,1)}, u32[]{:S(2)}) %copy-start) | copy-done | bytes 4194328
  10.1 0.0 copy-start.1
  10.1 1.6 %copy-done.1 = bf16[512,2048]{1,0:T(8,128)(2,1)S(1)} copy-done((bf16[512,2048]{1,0:T(8,128)(2,1)S(1)}, bf16[512,2048]{1,0:T(8,128)(2,1)}, u32[]{:S(2)}) %copy-start.1) | copy-done | bytes 2097176
  11.7 0.0 copy-start.2
  11.7 0.8 copy-done.2
  12.5 0.0 copy-start.3
  12.5 0.9 copy-done.3
  13.4 0.0 copy-start.4
  13.4 0.7 copy-done.4
  14.1 0.0 copy-start.5
  14.1 0.7 copy-done.5
  14.9 0.0 copy-start.6
  14.9 0.7 copy-done.6
  15.5 0.0 copy-start.7
  15.5 0.7 copy-done.7
  16.2 0.0 copy-start.8
  16.2 0.7 copy-done.8
  16.8 69.2 %shard_map.137 = (bf16[512,4096]{1,0:T(8,128)(2,1)S(1)}, bf16[16,512]{1,0:T(8,128)(2,1)S(1)}, f32[2,4096]{1,0:T(2,128)S(1)}, f32[16,6144]{1,0:T(8,128)S(1)}, f32[8,128]{1,0:T(8,128)S(1)}) custom-call(bf16[512,4096]{1,0:T(8,128)(2,1)S(1)} %copy-done, bf16[512,2048]{1,0:T(8,128)(2,1)S(1)} %copy-done.1, bf16[16,2048]{1,0:T(8,128)(2,1)S(1)} %bitcast.9, ...), custom_call_target="tpu_custom_call" | custom-call | tf_op jit(solution)/shard_map/pallas_call | solution.py:460
  86.0 0.0 copy-start.9
  86.0 0.6 slice.11
  86.6 1.2 slice.10
  87.7 2.7 %fusion = f32[512,2048]{1,0:T(8,128)} fusion(bf16[16,512]{1,0:T(8,128)(2,1)S(1)} %get-tuple-element.11, bf16[2048,16]{0,1:T(8,128)(2,1)S(1)} %copy-done.2), kind=kOutput, calls=%fused_computation.2 | convolution fusion | flops 33554432 | bytes 4276224 | tf_op jit(solution)/shard_map/dot_general | solution.py:25
  90.4 0.0 copy-done.9
  90.4 0.7 slice_bitcast_fusion
  91.1 7.9 %all-gather.2.cloned.1.call-done = bf16[2048,4096]{1,0:T(8,128)(2,1)} async-done(((bf16[64,4096]{1,0:T(8,128)(2,1)}), bf16[2048,4096]{1,0:T(8,128)(2,1)}) %all-gather.2.cloned.1.call-update) | async-done | bytes 16777232 | tf_op jit(solution)/shard_map/all_gather | solution.py:459
  99.0 15.2 %add_convert_fusion = bf16[512,2048]{1,0:T(8,128)(2,1)} fusion(f32[512,2048]{1,0:T(8,128)} %fusion, bf16[512,4096]{1,0:T(8,128)(2,1)} %copy-done.9, bf16[2048,4096]{1,0:T(8,128)(2,1)} %all-gather.2.cloned.1.call-done), kind=kOutput, calls=%fused_computation | convolution fusion | flops 8592031744 | bytes 27262976 | tf_op jit(solution)/shard_map/dot_general | solution.py:25
  114.2 0.6 copy.16
Async XLA Ops:
  7.2 91.8 %all-gather.2.cloned.1.call-start = ((), (), s32[]{:S(2)}) async-start(), calls=%async_computation | async-start | bytes 17301504 | tf_op jit(solution)/shard_map/all_gather | solution.py:459
  7.9 2.2 %copy-start = (bf16[512,4096]{1,0:T(8,128)(2,1)S(1)}, bf16[512,4096]{1,0:T(8,128)(2,1)}, u32[]{:S(2)}) copy-start(bf16[512,4096]{1,0:T(8,128)(2,1)} %hidden.1) | copy-start | bytes 12582916
  10.1 1.6 %copy-start.1 = (bf16[512,2048]{1,0:T(8,128)(2,1)S(1)}, bf16[512,2048]{1,0:T(8,128)(2,1)}, u32[]{:S(2)}) copy-start(bf16[512,2048]{1,0:T(8,128)(2,1)} %attn.1) | copy-start | bytes 6291460
  11.7 0.8 copy-start.2
  12.5 0.9 copy-start.3
  13.4 0.7 copy-start.4
  14.1 0.7 copy-start.5
  14.9 0.7 copy-start.6
  15.5 0.7 copy-start.7
  16.2 0.7 copy-start.8
  86.0 4.4 %copy-start.9 = (bf16[512,4096]{1,0:T(8,128)(2,1)}, bf16[512,4096]{1,0:T(8,128)(2,1)S(1)}, u32[]{:S(2)}) copy-start(bf16[512,4096]{1,0:T(8,128)(2,1)S(1)} %get-tuple-element.10) | copy-start | bytes 12582916
Sparse Core Ops, SparseCore 0:
  10.6 88.3 all-gather.1

commit v2 on v1

--- a/solution.py
+++ b/solution.py
@@ -11,6 +11,7 @@
 F32 = jnp.float32
 BF16 = jnp.bfloat16
 HI = lax.Precision.HIGHEST
+CUT = 3072
 NT = (((1,), (1,)), ((), ()))
 TN = (((0,), (0,)), ((), ()))
 
@@ -37,6 +38,24 @@
     nq,
     hidden,
     attn,
+    weight,
+    down_h,
+    up_h,
+    gain_h,
+    queries_h,
+    lengths_h,
+    offsets_h,
+    positives_h,
+    attn_out,
+    query_out,
+    down_out,
+    up_out,
+    loss_out,
+    hv,
+    av,
+    wv,
+    dyv,
+    ov,
     down_t,
     up,
     gain,
@@ -44,20 +63,13 @@
     lengths,
     offsets,
     positives,
-    dy_out,
-    blt_out,
-    query_out,
-    adapter_out,
-    loss_out,
-    hv,
-    av,
-    dyv,
     ub,
     eb,
     unit_s,
     pool_s,
     ssq_s,
     col_s,
+    bl_s,
     dn_s,
     lx,
     dpb,
@@ -69,7 +81,11 @@
     plane_in,
     z_in,
     total_s,
+    query_s,
+    loss_s,
+    sum_s,
     local_sem,
+    out_sem,
     u_send,
     u_recv,
     e_send,
@@ -90,6 +106,12 @@
     g_recv,
     s_send,
     s_recv,
+    w_send,
+    w_recv,
+    wz_send,
+    wz_recv,
+    wc_send,
+    wc_recv,
 ):
     nl = 2 * ng
     tok, width = hv.shape
@@ -159,10 +181,23 @@
 
         lax.fori_loop(1, n, body, 0)
 
-    load_hidden = pltpu.make_async_copy(hidden, hv, local_sem.at[0])
-    load_attn = pltpu.make_async_copy(attn, av, local_sem.at[1])
-    load_hidden.start()
-    load_attn.start()
+    def load(source, target, i):
+        copy = pltpu.make_async_copy(source, target, local_sem.at[i])
+        copy.start()
+        return copy
+
+    load_queries = load(queries_h, queries, 0)
+    load_positives = load(positives_h, positives, 1)
+    load_hidden = load(hidden, hv, 2)
+    load_weight = load(weight, wv.at[dp], 3)
+    load_rest = [
+        load(gain_h, gain, 4),
+        load(lengths_h, lengths, 5),
+        load(offsets_h, offsets, 6),
+    ]
+    load_attn = load(attn, av, 7)
+    load_down = load(down_h, down_t, 8)
+    load_up = load(up_h, up, 9)
 
     barrier = pltpu.get_barrier_semaphore()
 
@@ -177,6 +212,208 @@
     greet(nq, plane_peer)
     greet(nl, line_peer)
 
+    x_me = lax.rem(q_me, 4)
+    y_me = lax.div(q_me, 4)
+    parity = lax.rem(grp, 2)
+
+    def along(axis, o):
+        if axis == 0:
+            return 4 * y_me + lax.rem(x_me + o, 4)
+        return 4 * lax.rem(y_me + o, 4) + x_me
+
+    def w_rows(whose, part):
+        return pl.ds(pl.multiple_of(32 * whose + 16 * part, 16), 16)
+
+    def w_pieces(q, part):
+        d = 2 * q + core
+        pieces = [wv.at[d, w_rows(parity, part), :]]
+        if CUT < width:
+            pieces.append(wv.at[d, w_rows(1 - parity, part), CUT:])
+        return pieces
+
+    def w_copy(q, part, to, a, b):
+        for r, piece in enumerate(w_pieces(q, part)):
+            pltpu.make_async_remote_copy(
+                src_ref=piece,
+                dst_ref=piece,
+                send_sem=w_send.at[r, part, a, b],
+                recv_sem=w_recv.at[r, part, q],
+                device_id=(grp, 2 * to + core),
+                device_id_type=MESH,
+            ).start()
+
+    def w_wait(q, part):
+        for r, piece in enumerate(w_pieces(q, part)):
+            pltpu.make_async_remote_copy(
+                src_ref=piece,
+                dst_ref=piece,
+                send_sem=w_recv.at[r, part, q],
+                recv_sem=w_recv.at[r, part, q],
+                device_id=(grp, dp),
+                device_id_type=MESH,
+            ).wait_recv()
+
+    def w_own(part, b):
+        w_copy(q_me, part, along(part, b), 4, b)
+
+    def w_relay(part, a, b):
+        w_copy(along(part, a), part, along(1 - part, b), a, b)
+
+    def z_copies(q):
+        d = 2 * q + core
+        for part, o in ((0, ng - 1), (1, 1)):
+            piece = wv.at[d, w_rows(parity, part), 0:CUT]
+            yield pltpu.make_async_remote_copy(
+                src_ref=piece,
+                dst_ref=piece,
+                send_sem=wz_send.at[part, q],
+                recv_sem=wz_recv.at[part, q],
+                device_id=(lax.rem(grp + o, ng), dp),
+                device_id_type=MESH,
+            )
+
+    def w_across(q):
+        for copy in z_copies(q):
+            copy.start()
+
+    def w_across_wait(q):
+        d = 2 * q + core
+        for part in (0, 1):
+            piece = wv.at[d, w_rows(1 - parity, part), 0:CUT]
+            pltpu.make_async_remote_copy(
+                src_ref=piece,
+                dst_ref=piece,
+                send_sem=wz_recv.at[part, q],
+                recv_sem=wz_recv.at[part, q],
+                device_id=(grp, dp),
+                device_id_type=MESH,
+            ).wait_recv()
+
+    def core_copy(q, side):
+        chunk_ref = wv.at[2 * q + side]
+        return pltpu.make_async_remote_copy(
+            src_ref=chunk_ref,
+            dst_ref=chunk_ref,
+            send_sem=wc_send.at[q],
+            recv_sem=wc_recv.at[q],
+            device_id=(grp, 2 * q_me + 1 - core),
+            device_id_type=MESH,
+        )
+
+    def at(oy, ox):
+        return 4 * lax.rem(y_me + oy, 4) + lax.rem(x_me + ox, 4)
+
+    def w_step0():
+        load_weight.wait()
+        for b in (1, 3):
+            for part in (0, 1):
+                w_own(part, b)
+                w_relay(part, 0, b)
+        core_copy(q_me, core).start()
+
+    def w_step1():
+        for part in (0, 1):
+            w_own(part, 2)
+            w_relay(part, 0, 2)
+
+    def w_step2():
+        for part in (0, 1):
+            for a in (1, 3):
+                w_wait(along(part, a), part)
+        for a in (1, 3):
+            for b in (1, 3):
+                for part in (0, 1):
+                    w_relay(part, a, b)
+        for part in (0, 1):
+            for a in (1, 3):
+                w_wait(along(part, a), 1 - part)
+                w_across(along(part, a))
+
+    def w_step3():
+        for a in (1, 3):
+            for part in (0, 1):
+                w_relay(part, a, 2)
+
+    def w_step4():
+        for part in (0, 1):
+            w_wait(along(part, 2), part)
+        for b in (1, 2, 3):
+            for part in (0, 1):
+                w_relay(part, 2, b)
+
+    def w_step5():
+        for part in (0, 1):
+            w_wait(along(part, 2), 1 - part)
+            w_across(along(part, 2))
+        for oy in (1, 3):
+            for ox in (1, 3):
+                w_wait(at(oy, ox), 0)
+                w_wait(at(oy, ox), 1)
+                w_across(at(oy, ox))
+
+    def w_step6():
+        for oy, ox in ((1, 2), (3, 2), (2, 1), (2, 3), (2, 2)):
+            w_wait(at(oy, ox), 0)
+            w_wait(at(oy, ox), 1)
+            w_across(at(oy, ox))
+
+    def tile_at(t):
+        k = lax.div(t, 2)
+        oy = jnp.where(k == 2, 3, jnp.where(k == 3, 2, k))
+        near = lax.div(x_me, 2)
+        pair = lax.rem(near + lax.rem(t, 2), 2)
+        return 2 * lax.rem(y_me + oy, 4) + pair
+
+    def w_finish(q):
+        w_across_wait(q)
+        core_copy(q, core).start()
+
+    def tile_start(t):
+        n = tile_at(t)
+        w_finish(2 * n)
+        w_finish(2 * n + 1)
+
+    def tile(t, carry):
+        n = tile_at(t)
+        core_copy(2 * n, 1 - core).wait_recv()
+        core_copy(2 * n + 1, 1 - core).wait_recv()
+        columns = pl.ds(pl.multiple_of(256 * n, 256), 256)
+        w_tile = wv[pl.ds(4 * n, 4)].reshape(256, width)
+        out = mm(dyv[...], w_tile, NT) + mm(bl_s[:, 0:16], down_t[:, columns])
+        ov[:, columns] = out.astype(BF16)
+        pltpu.make_async_copy(ov.at[:, columns], attn_out.at[:, columns], out_sem.at[t]).start()
+        return carry
+
+    def tile_stored(t, carry):
+        columns = pl.ds(pl.multiple_of(256 * tile_at(t), 256), 256)
+        pltpu.make_async_copy(ov.at[:, columns], attn_out.at[:, columns], out_sem.at[t]).wait()
+        return carry
+
+    def w_drain():
+        for part in (0, 1):
+            for b in (1, 2, 3):
+                for a in (0, 1, 2, 3, 4):
+                    q = q_me if a == 4 else along(part, a)
+                    for r, piece in enumerate(w_pieces(q, part)):
+                        pltpu.make_async_remote_copy(
+                            src_ref=piece,
+                            dst_ref=piece,
+                            send_sem=w_send.at[r, part, a, b],
+                            recv_sem=w_send.at[r, part, a, b],
+                            device_id=(grp, dp),
+                            device_id_type=MESH,
+                        ).wait_send()
+
+        def body(o, carry):
+            q = lax.rem(q_me + o, nq)
+            for copy in z_copies(q):
+                copy.wait_send()
+            core_copy(q, core).wait_send()
+            return carry
+
+        lax.fori_loop(1, nq, body, 0)
+        core_copy(q_me, core).wait_send()
+
     odd16 = lax.rem(iota((16, 1), 0), 2) == 1
 
     def by_row(even, odd):
@@ -190,6 +427,8 @@
     def chunk(k):
         return slice(k * wc, (k + 1) * wc)
 
+    load_queries.wait()
+    load_positives.wait()
     for k in range(8):
         unit_s[2 * k : 2 * k + 2, :] = queries[:, chunk(k)].astype(F32)
     query16 = unit_s[...]
@@ -205,17 +444,24 @@
 
     pl.semaphore_wait(barrier, nq - 1 + nl - 1)
     fan_out(nl, line_peer, lambda there: ub.at[l_me], ub, l_me, u_send, u_recv)
+    w_step0()
 
     load_hidden.wait()
 
     def squares(i, carry):
         rows = pl.ds(pl.multiple_of(i * 16, 16), 16)
         v = hv[rows, :].astype(F32)
-        ssq_s[rows, :] = jnp.broadcast_to(jnp.sum(v * v, axis=1, keepdims=True), (16, 128))
+        v = v * v
+        total = v[:, 0:128]
+        for t in range(1, width // 128):
+            total = total + v[:, t * 128 : t * 128 + 128]
+        ssq_s[rows, :] = total
         return carry
 
-    lax.fori_loop(0, tok // 16, squares, 0)
-    ssq_row = jnp.transpose(ssq_s[...])[0:1, :]
+    lax.fori_loop(0, tok // 16, squares, 0, unroll=2)
+    ssq_row = mm(jnp.ones((8, 128), F32), ssq_s[...], NT, HI)[0:1, :]
+    for copy in load_rest:
+        copy.wait()
     rstd = lax.rsqrt(ssq_row * (1.0 / width) + 1e-05)
     token = iota((1, tok), 1)
     inside0 = (token >= offsets[0]) & (token < offsets[0] + lengths[0])
@@ -235,8 +481,11 @@
     embed = pooled / pnorm
     eb[q_me] = embed.astype(BF16)
     fan_out(nq, plane_peer, lambda there: eb.at[q_me], eb, q_me, e_send, e_recv)
+    w_step1()
 
     load_attn.wait()
+    load_down.wait()
+    load_up.wait()
     flt = mm(down_t[...], av[...], NT).astype(BF16)
     hut = mm(up[...], hv[...], NT)
     na, nb = 16 * nq, 16 * nl
@@ -278,6 +527,7 @@
     row8 = iota((8, 128), 0)
     lx[l_me] = jnp.where(row8 == 0, partial, jnp.where(row8 == 1, chosen, 0.0))
     fan_out(nl, line_peer, lambda there: lx.at[l_me], lx, l_me, x_send, x_recv)
+    w_step2()
     fan_wait(nl, line_peer, lx, l_me, x_recv)
     line = jnp.sum(lx[...], axis=0)
     lse = jnp.log(jnp.where(used, line[0:1, :], 1.0))
@@ -290,18 +540,18 @@
     dpb[:, :, wc:] = jnp.broadcast_to(jnp.where(iota((1, 1, 128), 2) == q_me, line_loss.reshape(1, 1, 1), 0.0), (nq, 16, 128))
     rb[q_me] = dpb[q_me]
     fan_out(nq, plane_peer, lambda there: dpb.at[there], rb, q_me, d_send, d_recv)
-    dub[...] = mm(jnp.transpose(g1).astype(BF16), ebm).reshape(nl, 16, wc)
+    w_step3()
+    w_step4()
+    dub[...] = mm(jnp.transpose(g1).astype(BF16), ebm).reshape(nl, 16, wc).astype(BF16)
     rub[l_me] = dub[l_me]
     fan_out(nl, line_peer, lambda there: dub.at[there], rub, l_me, v_send, v_recv)
 
     fan_wait(nq, plane_peer, rb, q_me, d_recv)
     gathered = jnp.sum(rb[...], axis=0)
-    loss_out[...] = jnp.broadcast_to(
-        jnp.sum(gathered[0:8, wc:], axis=1, keepdims=True) * (1.0 / passages), (8, 128)
-    )
+    loss_s[...] = jnp.sum(gathered[0:1, wc:], axis=1, keepdims=True) * (1.0 / passages)
     d_embed = 50.0 * gathered[:, 0:wc]
-    along = pair_sum(jnp.sum(embed * d_embed, axis=1, keepdims=True))
-    pool_s[...] = (d_embed - embed * along) / pnorm / counts
+    shared = pair_sum(jnp.sum(embed * d_embed, axis=1, keepdims=True))
+    pool_s[...] = (d_embed - embed * shared) / pnorm / counts
     dn_s[...] = jnp.zeros_like(dn_s)
     for k in range(8):
         dn = pool_s[2 * k : 2 * k + 2, :] * gain[0:1, chunk(k)]
@@ -321,7 +571,6 @@
     u0 = u3[:, 0:1] + u3[:, 2:3] + u3[:, 4:5]
     u1 = u3[:, 1:2] + u3[:, 3:4] + u3[:, 5:6]
     blt = (2.0 * (u0 * w0 + u1 * w1 - b * hut)).astype(BF16)
-    blt_out[...] = blt
     tiles_down, tiles_up = feat // 128, width // 128
     per = (tiles_down + tiles_up) // nq
 
@@ -340,9 +589,10 @@
     fbl = (fb - fbh.astype(F32)).astype(BF16)
     f0 = jnp.sum(w0 * fl, axis=1, keepdims=True)
     f1 = jnp.sum(w1 * fl, axis=1, keepdims=True)
+    fb2 = jnp.concatenate([fbh, fbl], axis=0)
     for k in range(8):
-        hk = hv[:, chunk(k)]
-        up2 = mm(fbh, hk) + mm(fbl, hk)
+        up2 = mm(fb2, hv[:, chunk(k)])
+        up2 = up2[0:16] + up2[16:32]
         up_part = 2.0 * (f0 * dn_s[8:9, chunk(k)] + f1 * dn_s[9:10, chunk(k)] - up2)
         for t in range(wc // 128):
             put(tiles_down + k * (wc // 128) + t, up_part[:, t * 128 : t * 128 + 128])
@@ -361,37 +611,45 @@
     )
     swap.start()
 
-    cols = jnp.where(
-        iota((128, tok), 0) == 0, w0, jnp.where(iota((128, tok), 0) == 1, w1, b)
-    )
-    col_s[...] = jnp.transpose(cols)
-    swap.wait()
+    w_step5()
+    swap.wait_recv()
     mine = half(core)
     core_in[...] = core_in[...] + ab[:, mine, :]
     plane_in[q_me] = core_in[q_me]
     fan_out(nq, plane_peer, lambda there: core_in.at[there], plane_in, q_me, p_send, p_recv)
 
+    row_id = iota((128, tok), 0)
+    col_s[...] = jnp.transpose(jnp.where(row_id == 0, w0 + w1, jnp.where(row_id == 1, b, 0.0)))
+    blf = jnp.concatenate([blt.astype(F32), jnp.zeros((112, tok), F32)], axis=0)
+    bl_s[...] = jnp.transpose(blf).astype(BF16)
+
     def rows_dy(i, carry):
         rows = pl.ds(pl.multiple_of(i * 16, 16), 16)
         c = col_s[rows, :]
-        v = hv[rows, :].astype(F32)
-        dyv[rows, :] = (c[:, 0:1] * dn_s[8:9, :] + c[:, 1:2] * dn_s[9:10, :] - c[:, 2:3] * v).astype(BF16)
+        second = jnp.where(i * 16 >= offsets[1], 1, 0)
+        dn_row = dn_s[pl.ds(8 + second, 1), :]
+        dyv[rows, :] = (c[:, 0:1] * dn_row - c[:, 1:2] * hv[rows, :].astype(F32)).astype(BF16)
         return carry
 
-    lax.fori_loop(0, tok // 16, rows_dy, 0)
-    store_dy = pltpu.make_async_copy(dyv, dy_out, local_sem.at[2])
-    store_dy.start()
+    lax.fori_loop(0, tok // 16, rows_dy, 0, unroll=2)
 
     fan_wait(nq, plane_peer, plane_in, q_me, p_recv)
     z_in[grp] = jnp.sum(plane_in[...], axis=0)
     fan_out(ng, z_peer, lambda there: z_in.at[grp], z_in, grp, z_send, z_recv)
+    w_step6()
 
     fan_wait(nl, line_peer, rub, l_me, v_recv)
-    d_unit = 50.0 * jnp.sum(rub[...], axis=0)
+    d_unit = 50.0 * jnp.sum(rub[...].astype(F32), axis=0)
     unit = unit_s[...]
     unit_s[...] = (d_unit - unit * pair_sum(jnp.sum(unit * d_unit, axis=1, keepdims=True))) / qnorm
     for k in range(8):
-        query_out[:, chunk(k)] = unit_s[2 * k : 2 * k + 2, :]
+        query_s[:, chunk(k)] = unit_s[2 * k : 2 * k + 2, :]
+    store_query = pltpu.make_async_copy(query_s, query_out, local_sem.at[10])
+    store_query.start()
+    store_loss = pltpu.make_async_copy(loss_s, loss_out, local_sem.at[11])
+    store_loss.start()
+    w_finish(4 * y_me + x_me + 1 - 2 * lax.rem(x_me, 2))
+    tile_start(1)
 
     fan_wait(ng, z_peer, z_in, grp, z_recv)
     total_s[q_me, mine, :] = jnp.sum(z_in[...], axis=0)
@@ -418,10 +676,13 @@
             recv_sem=g_recv.at[there],
             device_id=device,
             device_id_type=MESH,
-        ).wait()
+        ).wait_recv()
         return carry
 
     lax.fori_loop(1, nq, gather_piece, 0)
+    tile(0, 0)
+    tile_start(2)
+    tile(1, 0)
     lax.fori_loop(1, nq, gather_wait, 0)
     back = pltpu.make_async_remote_copy(
         src_ref=total_s.at[:, mine, :],
@@ -432,6 +693,23 @@
         device_id_type=MESH,
     )
     back.start()
+
+    def tiles(t, carry):
+        tile_start(t + 1)
+        return tile(t, carry)
+
+    lax.fori_loop(2, 7, tiles, 0)
+    tile(7, 0)
+
+    back.wait_recv()
+    for t in range(tiles_down):
+        sum_s[:, t * 128 : t * 128 + 128] = get(total_s, t)
+    for t in range(tiles_up):
+        sum_s[:, feat + t * 128 : feat + t * 128 + 128] = get(total_s, tiles_down + t)
+    store_down = pltpu.make_async_copy(sum_s.at[:, 0:feat], down_out, local_sem.at[12])
+    store_down.start()
+    store_up = pltpu.make_async_copy(sum_s.at[:, feat:], up_out, local_sem.at[13])
+    store_up.start()
     fan_drain(nl, line_peer, lambda there: ub.at[there], u_send)
     fan_drain(nq, plane_peer, lambda there: eb.at[there], e_send)
     fan_drain(nl, line_peer, lambda there: lx.at[there], x_send)
@@ -439,10 +717,15 @@
     fan_drain(nl, line_peer, lambda there: dub.at[there], v_send)
     fan_drain(nq, plane_peer, lambda there: core_in.at[there], p_send)
     fan_drain(ng, z_peer, lambda there: z_in.at[there], z_send)
-    store_dy.wait()
-    back.wait()
-    for t in range(tiles_down + tiles_up):
-        adapter_out[:, t * 128 : t * 128 + 128] = get(total_s, t)
+    fan_drain(nq, plane_peer, lambda there: core_in.at[there], g_send)
+    swap.wait_send()
+    back.wait_send()
+    w_drain()
+    store_query.wait()
+    store_loss.wait()
+    store_down.wait()
+    store_up.wait()
+    lax.fori_loop(0, 8, tile_stored, 0)
 
 
 def per_device(ng, nq, attn, hidden, weight, down, up, gain, queries, lengths, offsets, positives):
@@ -451,45 +734,56 @@
     wc = width // 8
     nl = 2 * ng
     piece = (feat + width) // nq
-    down_t = down.T
-    vmem = pl.BlockSpec(memory_space=pltpu.VMEM)
-    smem = pl.BlockSpec(memory_space=pltpu.SMEM)
-    anywhere = pl.BlockSpec(memory_space=pl.ANY)
+    hbm = pl.BlockSpec(memory_space=pltpu.HBM)
     dma = pltpu.SemaphoreType.DMA
-    everything = lax.all_gather(weight, "dp", axis=0, tiled=True)
-    dy, blt, query_gradient, adapters, loss = pl.pallas_call(
+    outs = (
+        jax.ShapeDtypeStruct((tok, feat), BF16),
+        jax.ShapeDtypeStruct((2, width), F32),
+        jax.ShapeDtypeStruct((16, feat), F32),
+        jax.ShapeDtypeStruct((16, width), F32),
+        jax.ShapeDtypeStruct((1, 1), F32),
+    )
+    results = pl.pallas_call(
         functools.partial(kernel, ng, nq),
-        out_shape=(
-            jax.ShapeDtypeStruct((tok, width), BF16),
-            jax.ShapeDtypeStruct((16, tok), BF16),
-            jax.ShapeDtypeStruct((2, width), F32),
-            jax.ShapeDtypeStruct((16, feat + width), F32),
-            jax.ShapeDtypeStruct((8, 128), F32),
-        ),
-        in_specs=[anywhere, anywhere, vmem, vmem, vmem, vmem, smem, smem, smem],
-        out_specs=(anywhere, vmem, vmem, vmem, vmem),
+        out_shape=outs,
+        in_specs=[hbm] * 10,
+        out_specs=(hbm,) * 5,
         scratch_shapes=[
             pltpu.VMEM((tok, width), BF16),
             pltpu.VMEM((tok, feat), BF16),
+            pltpu.VMEM((2 * nq, 64, width), BF16),
             pltpu.VMEM((tok, width), BF16),
+            pltpu.VMEM((tok, feat), BF16),
+            pltpu.VMEM((16, feat), BF16),
+            pltpu.VMEM((16, width), BF16),
+            pltpu.VMEM((1, width), F32),
+            pltpu.VMEM((2, width), BF16),
+            pltpu.SMEM((2,), jnp.int32),
+            pltpu.SMEM((2,), jnp.int32),
+            pltpu.SMEM((2,), jnp.int32),
             pltpu.VMEM((nl, 16, wc + 128), BF16),
             pltpu.VMEM((nq, 16, wc), BF16),
             pltpu.VMEM((16, wc), F32),
             pltpu.VMEM((16, wc), F32),
             pltpu.VMEM((tok, 128), F32),
             pltpu.VMEM((tok, 128), F32),
+            pltpu.VMEM((tok, 128), BF16),
             pltpu.VMEM((16, width), F32),
             pltpu.VMEM((nl, 8, 128), F32),
             pltpu.VMEM((nq, 16, wc + 128), F32),
             pltpu.VMEM((nq, 16, wc + 128), F32),
-            pltpu.VMEM((nl, 16, wc), F32),
-            pltpu.VMEM((nl, 16, wc), F32),
+            pltpu.VMEM((nl, 16, wc), BF16),
+            pltpu.VMEM((nl, 16, wc), BF16),
             pltpu.VMEM((nq, 16, piece), F32),
             pltpu.VMEM((nq, 8, piece), F32),
             pltpu.VMEM((nq, 8, piece), F32),
             pltpu.VMEM((ng, 8, piece), F32),
             pltpu.VMEM((nq, 16, piece), F32),
-            dma((3,)),
+            pltpu.VMEM((2, width), F32),
+            pltpu.VMEM((1, 1), F32),
+            pltpu.VMEM((16, feat + width), F32),
+            dma((14,)),
+            dma((8,)),
             dma((nl,)),
             dma((nl,)),
             dma((nq,)),
@@ -510,21 +804,19 @@
             dma((nq,)),
             dma,
             dma,
+            dma((2, 2, 5, 4)),
+            dma((2, 2, nq)),
+            dma((2, nq)),
+            dma((2, nq)),
+            dma((nq,)),
+            dma((nq,)),
         ],
         compiler_params=pltpu.CompilerParams(
-            collective_id=0, has_side_effects=True, vmem_limit_bytes=40 * 1024 * 1024
+            collective_id=0, has_side_effects=True, vmem_limit_bytes=56 * 1024 * 1024
         ),
-    )(hidden, attn, down_t, up, gain.reshape(1, width), queries, lengths, offsets, positives)
-    attention_gradient = (
-        mm(dy, everything, NT) + mm(blt, down_t, TN)
-    ).astype(BF16)
-    return (
-        attention_gradient,
-        query_gradient,
-        adapters[:, 0:feat].T,
-        adapters[:, feat:],
-        loss[0, 0],
-    )
+    )(hidden, attn, weight, down.T, up, gain.reshape(1, width), queries, lengths, offsets, positives)
+    attention, query, down_sum, up_sum, loss = results
+    return attention, query, down_sum.T, up_sum, loss.reshape(())
 
 
 def solution(mesh):

time: 122 us -> 107 us (0.88)
  Pallas kernels: 69.2 us -> 99 us
  matrix products: 17.9 us -> 0 us
  between operations: 14.1 us -> 2.37 us
  waiting for transfers between devices: 8.57 us -> 0 us
  local copies, waits for them, and re-layouts: 11.9 us -> 5.19 us
    pallas_call x1, Pallas kernels: 69.2 us -> 99 us  [per_device(): pl.pallas_call(functools.partial(kernel, ng, nq), out_shape=outs, in_spec...]
    dot_general x2 -> x0, matrix products: 17.9 us -> none  [mm(): lax.dot_general(a, b, dims, precision=precision, preferred_element_type=F32)]
    all_gather x1 -> x0, waiting for transfers between devices: 7.89 us -> none  [per_device(): everything = lax.all_gather(weight, 'dp', axis=0, tiled=True)]
    unnamed x21 -> x10, local copies, waits for them, and re-layouts: 9.53 us -> 5.19 us
    slice x2 -> x0, local copies, waits for them, and re-layouts: 1.72 us -> none  [the longest x1 1.16 us: per_device(): adapters[:, feat:]]
  transfers between devices with their start and end apart: 1 -> 0, of which waited for: 1 -> 0; matrix products, arithmetic and copies ran while one was open for 4% -> 0% of each run, Pallas kernels for 57% -> 0%
where the time goes in v2:
time: 107 us
  Pallas kernels  99 us (93%)
  local copies, waits for them, and re-layouts  5.19 us (5%)
  between operations  2.37 us (2%)
    pallas_call x1, Pallas kernels, per_device(): pl.pallas_call(functools.partial(kernel, ng, nq), out_shape=outs, in_spec...  99 us
    unnamed x10, local copies, waits for them, and re-layouts  5.19 us

profile of v2, /device:TPU:1, one launch (start us, length us, event | category | flops | bytes accessed | tf_op | source)
XLA Modules:
  0.0 106.6 jit_solution(10168926682069251781)
XLA Ops:
  0.6 99.0 %shard_map.137 = (bf16[512,2048]{1,0:T(8,128)(2,1)}, f32[2,4096]{1,0:T(2,128)}, f32[16,2048]{1,0:T(8,128)}, f32[16,4096]{1,0:T(8,128)}, f32[1,1]{1,0:T(1,128)}) custom-call(bf16[512,4096]{1,0:T(8,128)(2,1)} %hidden.1, bf16[512,2048]{1,0:T(8,128)(2,1)} %attn.1, bf16[64,4096]{1,0:T(8,128)(2,1)} %weight.1, bf16[16,2048]{1,0:T(8,128)(2,1)} %bitcast.5, ...), custom_call_target="tpu_custom_call" | custom-call | tf_op jit(solution)/shard_map/pallas_call | solution.py:746
  99.6 0.0 copy-start.2
  99.6 0.0 copy-start.1
  99.7 0.0 copy-start
  99.7 3.2 %copy.20 = bf16[512,2048]{1,0:T(8,128)(2,1)} copy(bf16[512,2048]{1,0:T(8,128)(2,1)} %get-tuple-element.20) | data formatting | bytes 4194304
  102.9 0.0 copy-done.2
  102.9 0.6 copy.21
  103.5 0.0 copy-done.1
  103.5 0.7 copy.22
  104.2 0.0 copy-done
  104.2 0.7 copy.23
Async XLA Ops:
  99.6 3.2 %copy-start.2 = (f32[2,4096]{1,0:T(2,128)S(1)}, f32[2,4096]{1,0:T(2,128)}, u32[]{:S(2)}) copy-start(f32[2,4096]{1,0:T(2,128)} %get-tuple-element.21) | copy-start | bytes 98308
  99.6 3.8 %copy-start.1 = (f32[16,2048]{1,0:T(8,128)S(1)}, f32[16,2048]{1,0:T(8,128)}, u32[]{:S(2)}) copy-start(f32[16,2048]{1,0:T(8,128)} %get-tuple-element.12) | copy-start | bytes 393220
  99.7 4.5 %copy-start = (f32[16,4096]{1,0:T(8,128)S(1)}, f32[16,4096]{1,0:T(8,128)}, u32[]{:S(2)}) copy-start(f32[16,4096]{1,0:T(8,128)} %get-tuple-element.23) | copy-start | bytes 786436

commit v3 on v2

v3 whole, which is shorter than its diff:
```python
import functools

import jax
import jax.numpy as jnp
from jax import lax
from jax.experimental import pallas as pl
from jax.experimental.pallas import tpu as pltpu
from jax.sharding import PartitionSpec as P

MESH = pl.DeviceIdType.MESH
F32 = jnp.float32
BF16 = jnp.bfloat16
HI = lax.Precision.HIGHEST
NT = (((1,), (1,)), ((), ()))
TN = (((0,), (0,)), ((), ()))


def iota(shape, dim):
    return lax.broadcasted_iota(jnp.int32, shape, dim)


def mm(a, b, dims=None, precision=None):
    if dims is None:
        dims = (((1,), (0,)), ((), ()))
    return lax.dot_general(a, b, dims, precision=precision, preferred_element_type=F32)


def split3(x):
    high = x.astype(BF16).astype(F32)
    rest = x - high
    mid = rest.astype(BF16).astype(F32)
    return high, mid, (rest - mid).astype(BF16).astype(F32)


def kernel(
    ng,
    nq,
    hidden,
    attn,
    weight,
    down_h,
    up_h,
    gain_h,
    queries_h,
    lengths_h,
    offsets_h,
    positives_h,
    attn_out,
    query_out,
    down_out,
    up_out,
    loss_out,
    hv,
    av,
    wv,
    dyv,
    down_t,
    up,
    gain,
    queries,
    lengths,
    offsets,
    positives,
    ub,
    eb,
    unit_s,
    pool_s,
    ssq_s,
    col_s,
    bl_s,
    dn_s,
    lx,
    ll,
    dpb,
    rb,
    dub,
    rub,
    ab,
    core_in,
    plane_in,
    z_in,
    total_s,
    local_sem,
    u_sems,
    e_sems,
    x_sems,
    d_sems,
    v_sems,
    l_sems,
    c_send,
    c_recv,
    p_sems,
    z_sems,
    g_sems,
    s_send,
    s_recv,
    w_send,
    w_recv,
    wz_send,
    wz_recv,
    wc_send,
    wc_recv,
):
    nl = 2 * ng
    tok, width = hv.shape
    wc = width // 8
    feat = av.shape[1]
    passages = 2 * nl * nq
    middle = width // 2
    grp = lax.axis_index("grp")
    dp = lax.axis_index("dp")
    core = lax.rem(dp, 2)
    q_me = lax.div(dp, 2)
    l_me = 2 * grp + core

    def plane_peer(o):
        q = lax.rem(q_me + o, nq)
        return q, (grp, 2 * q + core)

    def line_peer(o):
        l = lax.rem(l_me + o, nl)
        return l, (lax.div(l, 2), 2 * q_me + lax.rem(l, 2))

    def z_peer(o):
        z = lax.rem(grp + o, ng)
        return z, (z, dp)

    def fan_out(n, peer, source, target, me, sems):
        def body(o, carry):
            there, device = peer(o)
            pltpu.make_async_remote_copy(
                src_ref=source(there),
                dst_ref=target.at[me],
                send_sem=sems.at[0],
                recv_sem=sems.at[1],
                device_id=device,
                device_id_type=MESH,
            ).start()
            return carry

        lax.fori_loop(1, n, body, 0)

    def amount(ref, sems):
        return pltpu.make_async_remote_copy(
            src_ref=ref,
            dst_ref=ref,
            send_sem=sems.at[0],
            recv_sem=sems.at[1],
            device_id=(grp, dp),
            device_id_type=MESH,
        )

    def fan_wait(n, target, sems):
        amount(target.at[0 : n - 1], sems).wait_recv()

    def fan_drain(n, target, sems):
        amount(target.at[0 : n - 1], sems).wait_send()

    def load(source, target, i):
        copy = pltpu.make_async_copy(source, target, local_sem.at[i])
        copy.start()
        return copy

    load_queries = load(queries_h, queries, 0)
    load_positives = load(positives_h, positives, 1)
    load_hidden = load(hidden, hv, 2)
    load_weight = load(weight, wv.at[dp], 3)
    load_rest = [
        load(gain_h, gain, 4),
        load(lengths_h, lengths, 5),
        load(offsets_h, offsets, 6),
    ]
    load_attn = load(attn, av, 7)
    load_down = load(down_h, down_t, 8)
    load_up = load(up_h, up, 9)

    barrier = pltpu.get_barrier_semaphore()

    def greet(n, peer):
        def body(o, carry):
            _, device = peer(o)
            pl.semaphore_signal(barrier, inc=1, device_id=device, device_id_type=MESH)
            return carry

        lax.fori_loop(1, n, body, 0)

    greet(nq, plane_peer)
    greet(nl, line_peer)

    x_me = lax.rem(q_me, 4)
    y_me = lax.div(q_me, 4)
    parity = lax.rem(grp, 2)

    def along(axis, o):
        if axis == 0:
            return 4 * y_me + lax.rem(x_me + o, 4)
        return 4 * lax.rem(y_me + o, 4) + x_me

    def w_rows(whose, part):
        return pl.ds(pl.multiple_of(32 * whose + 16 * part, 16), 16)

    def w_pieces(q, part, side):
        d = 2 * q + core
        first, last = ((0, 1), (0, 0.5), (0.5, 1))[side]

        def columns(start):
            size = width - start
            return pl.ds(start + int(first * size), int((last - first) * size))

        return (
            wv.at[d, w_rows(parity, part), columns(0)],
            wv.at[d, w_rows(1 - parity, part), columns(middle)],
        )

    def w_copy(q, part, axis, hop, side):
        for piece in w_pieces(q, part, side):
            pltpu.make_async_remote_copy(
                src_ref=piece,
                dst_ref=piece,
                send_sem=w_send.at[0 if side == 0 else 1],
                recv_sem=w_recv.at[part, side, q],
                device_id=(grp, 2 * along(axis, 1 if hop % 2 == 0 else 3) + core),
                device_id_type=MESH,
            ).start()

    def taken(ref, sem):
        return pltpu.make_async_remote_copy(
            src_ref=ref, dst_ref=ref, send_sem=sem, recv_sem=sem, device_id=(grp, dp), device_id_type=MESH
        )

    def w_wait_side(q, part, side):
        size = width // 2 if side == 0 else width // 4
        taken(wv.at[0, 0:48, 0:size], w_recv.at[part, side, q]).wait_recv()

    def at(oy, ox):
        return 4 * lax.rem(y_me + oy, 4) + lax.rem(x_me + ox, 4)

    def spot(part, o_first, o_second):
        return at(o_second, o_first) if part == 0 else at(o_first, o_second)

    def w_near(part, stage, o):
        axis = part if stage == 0 else 1 - part
        q = q_me if stage == 0 else spot(part, o, 0)
        for hop in (0, 1):
            w_copy(q, part, axis, hop, 0)

    def w_far(part, stage, o):
        axis = part if stage == 0 else 1 - part
        for hop, side, back_one in ((2, 1, 3), (3, 2, 1)):
            q = spot(part, back_one, 0) if stage == 0 else spot(part, o, back_one)
            w_copy(q, part, axis, hop, side)

    def w_wait(part, o_first, o_second):
        q = spot(part, o_first, o_second)
        last = o_first if o_second == 0 else o_second
        if last == 2:
            w_wait_side(q, part, 1)
            w_wait_side(q, part, 2)
        else:
            w_wait_side(q, part, 0)

    def z_copies(q):
        d = 2 * q + core
        for part, o in ((0, ng - 1), (1, 1)):
            piece = wv.at[d, w_rows(parity, part), 0:middle]
            yield pltpu.make_async_remote_copy(
                src_ref=piece,
                dst_ref=piece,
                send_sem=wz_send,
                recv_sem=wz_recv.at[q],
                device_id=(lax.rem(grp + o, ng), dp),
                device_id_type=MESH,
            )

    def w_across(q):
        for copy in z_copies(q):
            copy.start()

    def w_across_wait(q):
        taken(wv.at[0, 0:32, 0:middle], wz_recv.at[q]).wait_recv()

    def core_copies(q, side, pieces):
        d = 2 * q + side
        mine, rest = pl.ds(pl.multiple_of(32 * parity, 32), 32), pl.ds(pl.multiple_of(32 - 32 * parity, 32), 32)
        views = (
            wv.at[d, mine, :],
            wv.at[d, rest, middle:],
            wv.at[d, rest, 0:middle],
        )
        return [
            pltpu.make_async_remote_copy(
                src_ref=views[r],
                dst_ref=views[r],
                send_sem=wc_send,
                recv_sem=wc_recv.at[0 if r < 2 else 1, q],
                device_id=(grp, 2 * q_me + 1 - core),
                device_id_type=MESH,
            )
            for r in pieces
        ]

    def w_arrived(q):
        w_across(q)
        for copy in core_copies(q, core, (0, 1)):
            copy.start()

    def w_step0():
        load_weight.wait()
        for part in (0, 1):
            w_near(part, 0, 0)

    def w_step1():
        for part in (0, 1):
            w_near(part, 1, 0)
        for copy in core_copies(q_me, core, (0, 1, 2)):
            copy.start()
        for part in (0, 1):
            w_wait(part, 1, 0)
            w_wait(part, 3, 0)
            w_far(part, 0, 0)

    def w_step2():
        for part in (0, 1):
            w_near(part, 1, 1)
            w_near(part, 1, 3)
        for part in (0, 1):
            w_wait(part, 0, 1)
            w_wait(part, 0, 3)
        for oy, ox in ((0, 1), (0, 3), (1, 0), (3, 0)):
            w_arrived(at(oy, ox))

    def w_step3():
        for part in (0, 1):
            w_far(part, 1, 0)
            w_wait(part, 2, 0)
            w_near(part, 1, 2)
        for part in (0, 1):
            for o in (1, 3):
                w_wait(part, o, 1)
                w_wait(part, o, 3)
                w_far(part, 1, o)

    def w_step4():
        for part in (0, 1):
            w_wait(part, 2, 1)
            w_wait(part, 2, 3)
            w_far(part, 1, 2)
        for part in (0, 1):
            w_wait(part, 0, 2)
        for oy, ox in ((0, 2), (2, 0), (1, 1), (1, 3), (3, 1), (3, 3)):
            w_arrived(at(oy, ox))

    def w_step5():
        for part in (0, 1):
            w_wait(part, 1, 2)
            w_wait(part, 3, 2)
            w_wait(part, 2, 2)
        for oy, ox in ((1, 2), (3, 2), (2, 1), (2, 3), (2, 2)):
            w_arrived(at(oy, ox))

    def tile_at(t):
        def pick(values):
            out = values[0]
            for i, value in enumerate(values):
                out = jnp.where(t == i, value, out)
            return out

        oy = pick((0, 0, 1, 3, 1, 3, 2, 2))
        near = lax.div(x_me, 2)
        pair = lax.rem(near + pick((0, 1, 0, 0, 1, 1, 0, 1)), 2)
        return 2 * lax.rem(y_me + oy, 4) + pair

    def w_finish(q):
        w_across_wait(q)
        for copy in core_copies(q, core, (2,)):
            copy.start()

    def tile_start(t):
        n = tile_at(t)
        w_finish(2 * n)
        w_finish(2 * n + 1)

    def tile(t, carry):
        n = tile_at(t)
        for q in (2 * n, 2 * n + 1):
            taken(wv.at[0, 0:48, :], wc_recv.at[0, q]).wait_recv()
            taken(wv.at[0, 0:32, 0:middle], wc_recv.at[1, q]).wait_recv()
        columns = pl.ds(pl.multiple_of(256 * n, 256), 256)
        w_tile = wv[pl.ds(4 * n, 4)].reshape(256, width)
        out = mm(dyv[...], w_tile, NT) + mm(bl_s[:, 0:16], down_t[:, columns])
        attn_out[:, columns] = out.astype(BF16)
        return carry

    def w_drain():
        taken(wv.at[0:15, 0:32, :], w_send.at[0]).wait_send()
        taken(wv.at[0:15, 0:16, :], w_send.at[1]).wait_send()
        taken(wv.at[0:15, 0:16, :], wz_send).wait_send()
        taken(wv.at[0:16], wc_send).wait_send()

    odd16 = lax.rem(iota((16, 1), 0), 2) == 1

    def by_row(even, odd):
        return jnp.where(odd16, odd, even)

    def pair_sum(x):
        even = jnp.sum(jnp.where(odd16, 0.0, x), axis=0, keepdims=True)
        odd = jnp.sum(jnp.where(odd16, x, 0.0), axis=0, keepdims=True)
        return by_row(even, odd)

    def chunk(k):
        return slice(k * wc, (k + 1) * wc)

    load_queries.wait()
    load_positives.wait()
    for k in range(8):
        unit_s[2 * k : 2 * k + 2, :] = queries[:, chunk(k)].astype(F32)
    query16 = unit_s[...]
    qnorm = jnp.sqrt(pair_sum(jnp.sum(query16 * query16, axis=1, keepdims=True)) + 1e-06)
    unit16 = query16 / qnorm
    unit_s[...] = unit16
    ub[l_me, :, 0:wc] = unit16.astype(BF16)
    place = jnp.broadcast_to(by_row(positives[0], positives[1]), (16, 128))
    lane16 = iota((16, 128), 1)
    high_place = lax.shift_right_logical(place, 4)
    digits = jnp.where(lane16 == 0, high_place, jnp.where(lane16 == 1, place - 16 * high_place, 0))
    ub[l_me, :, wc:] = digits.astype(F32).astype(BF16)

    pl.semaphore_wait(barrier, nq - 1 + nl - 1)
    fan_out(nl, line_peer, lambda there: ub.at[l_me], ub, l_me, u_sems)
    w_step0()

    load_hidden.wait()

    def squares(i, carry):
        rows = pl.ds(pl.multiple_of(i * 16, 16), 16)
        v = hv[rows, :].astype(F32)
        v = v * v
        total = v[:, 0:128]
        for t in range(1, width // 128):
            total = total + v[:, t * 128 : t * 128 + 128]
        ssq_s[rows, :] = total
        return carry

    lax.fori_loop(0, tok // 16, squares, 0, unroll=2)
    ssq_row = mm(jnp.ones((8, 128), F32), ssq_s[...], NT, HI)[0:1, :]
    for copy in load_rest:
        copy.wait()
    rstd = lax.rsqrt(ssq_row * (1.0 / width) + 1e-05)
    token = iota((1, tok), 1)
    inside0 = (token >= offsets[0]) & (token < offsets[0] + lengths[0])
    inside1 = (token >= offsets[1]) & (token < offsets[1] + lengths[1])
    w0 = jnp.where(inside0, rstd, 0.0)
    w1 = jnp.where(inside1, rstd, 0.0)
    counts = by_row(lengths[0].astype(F32), lengths[1].astype(F32))
    row16 = iota((16, 1), 0)
    wh, wm, wl = split3(jnp.where(odd16, w1, w0))
    part = lax.div(row16, 2)
    w3 = jnp.where(part == 0, wh, jnp.where(part == 1, wm, jnp.where(part == 2, wl, 0.0))).astype(BF16)
    for k in range(8):
        p = mm(w3, hv[:, chunk(k)])
        pool_s[2 * k : 2 * k + 2, :] = (p[0:2] + p[2:4] + p[4:6]) * gain[0:1, chunk(k)]
    pooled = pool_s[...] / counts
    pnorm = jnp.sqrt(pair_sum(jnp.sum(pooled * pooled, axis=1, keepdims=True)) + 1e-06)
    embed = pooled / pnorm
    eb[q_me] = embed.astype(BF16)
    fan_out(nq, plane_peer, lambda there: eb.at[q_me], eb, q_me, e_sems)
    w_step1()

    load_attn.wait()
    load_down.wait()
    load_up.wait()
    flt = mm(down_t[...], av[...], NT).astype(BF16)
    hut = mm(up[...], hv[...], NT)
    na, nb = 16 * nq, 16 * nl
    np_, nqr = 2 * nq, 2 * nl

    def spread(rows, cols, row_is_block):
        small = iota((rows, cols), 0 if row_is_block else 1)
        big = iota((rows, cols), 1 if row_is_block else 0)
        return small == 2 * lax.div(big, 16) + lax.rem(big, 2)

    def as_f32(m):
        return jnp.where(m, 1.0, 0.0)

    same_chunk = lax.div(lax.rem(iota((na, nb), 0), 16), 2) == lax.div(lax.rem(iota((na, nb), 1), 16), 2)
    gather_a = as_f32(spread(np_, na, True))
    gather_b = as_f32(spread(nb, 128, False))
    first_b = as_f32(spread(nb, 128, False) & (lax.rem(iota((nb, 128), 0), 16) < 2))
    scatter_a = as_f32(spread(na, np_, False)).astype(BF16)
    scatter_b = as_f32(spread(128, nb, True)).astype(BF16)

    fan_wait(nl, ub, u_sems)
    ubm = ub[:, :, 0:wc].reshape(nb, wc)
    digit = as_f32(iota((16, 128), 0) == iota((16, 128), 1)).astype(BF16)
    place_b = mm(digit, ub[:, :, wc:].reshape(nb, 128), NT).astype(BF16)
    place_i = mm(place_b, first_b.astype(BF16))
    pos = 16.0 * place_i[0:1, :] + place_i[1:2, :]
    passage = iota((np_, 1), 0)
    number = 2 * (grp * 2 * nq + 2 * lax.div(passage, 2) + core) + lax.rem(passage, 2)
    used = iota((1, 128), 1) < nqr
    target = jnp.where((number.astype(F32) == pos) & used, 1.0, 0.0)

    fan_wait(nq, eb, e_sems)
    ebm = eb[...].reshape(na, wc)
    products = jnp.where(same_chunk, mm(ebm, ubm, NT), 0.0)
    logits = 50.0 * mm(mm(gather_a, products, precision=HI), gather_b, precision=HI)
    expo = jnp.where(used, jnp.exp(logits), 0.0)
    partial = jnp.sum(expo, axis=0, keepdims=True)
    chosen = jnp.sum(logits * target, axis=0, keepdims=True)
    row8 = iota((8, 128), 0)
    lx[l_me] = jnp.where(row8 == 0, partial, jnp.where(row8 == 1, chosen, 0.0))
    fan_out(nl, line_peer, lambda there: lx.at[l_me], lx, l_me, x_sems)
    w_step2()
    fan_wait(nl, lx, x_sems)
    line = jnp.sum(lx[...], axis=0)
    lse = jnp.log(jnp.where(used, line[0:1, :], 1.0))
    line_loss = jnp.sum(jnp.where(used, lse - line[1:2, :], 0.0), axis=1, keepdims=True)
    prob = jnp.exp(logits - lse)
    grad = jnp.where(used, (prob - target) * 1024.0, 0.0).astype(BF16)
    spread_grad = mm(mm(scatter_a, grad).astype(BF16), scatter_b)
    g1 = jnp.where(same_chunk, spread_grad, 0.0)
    dpb[...] = mm(g1.astype(BF16), ubm).reshape(nq, 16, wc).astype(BF16)
    rb[q_me] = dpb[q_me]
    fan_out(nq, plane_peer, lambda there: dpb.at[there], rb, q_me, d_sems)
    ll[q_me] = jnp.broadcast_to(line_loss, (8, 128))
    fan_out(nq, plane_peer, lambda there: ll.at[q_me], ll, q_me, l_sems)
    w_step3()
    dub[...] = mm(jnp.transpose(g1).astype(BF16), ebm).reshape(nl, 16, wc).astype(BF16)
    rub[l_me] = dub[l_me]
    fan_out(nl, line_peer, lambda there: dub.at[there], rub, l_me, v_sems)

    fan_wait(nq, rb, d_sems)
    d_embed = 50.0 * jnp.sum(rb[...].astype(F32), axis=0)
    shared = pair_sum(jnp.sum(embed * d_embed, axis=1, keepdims=True))
    pool_s[...] = (d_embed - embed * shared) / pnorm / counts
    dn_s[...] = jnp.zeros_like(dn_s)
    for k in range(8):
        dn = pool_s[2 * k : 2 * k + 2, :] * gain[0:1, chunk(k)]
        dh, dm, dl = split3(dn)
        dn_s[0:2, chunk(k)] = dh
        dn_s[2:4, chunk(k)] = dm
        dn_s[4:6, chunk(k)] = dl
        dn_s[8:10, chunk(k)] = dn
    dn3 = jnp.where(row16 < 6, dn_s[...], 0.0).astype(BF16)

    s3 = mm(dn3, hv[...], NT)
    s0 = s3[0:1] + s3[2:3] + s3[4:5]
    s1 = s3[1:2] + s3[3:4] + s3[5:6]
    s = jnp.where(inside0, s0, jnp.where(inside1, s1, 0.0))
    b = rstd * rstd * rstd * s * (1.0 / width)
    u3 = mm(up[...], dn3, NT)
    u0 = u3[:, 0:1] + u3[:, 2:3] + u3[:, 4:5]
    u1 = u3[:, 1:2] + u3[:, 3:4] + u3[:, 5:6]
    blt = (2.0 * (u0 * w0 + u1 * w1 - b * hut)).astype(BF16)
    tiles_down, tiles_up = feat // 128, width // 128
    per = (tiles_down + tiles_up) // nq

    def put(t, x):
        ab[t // per, :, (t % per) * 128 : (t % per) * 128 + 128] = x

    def get(ref, t):
        return ref[t // per, :, (t % per) * 128 : (t % per) * 128 + 128]

    down_part = mm(blt, av[...])
    for t in range(tiles_down):
        put(t, down_part[:, t * 128 : t * 128 + 128])
    fl = flt.astype(F32)
    fb = b * fl
    fbh = fb.astype(BF16)
    fbl = (fb - fbh.astype(F32)).astype(BF16)
    f0 = jnp.sum(w0 * fl, axis=1, keepdims=True)
    f1 = jnp.sum(w1 * fl, axis=1, keepdims=True)
    fb2 = jnp.concatenate([fbh, fbl], axis=0)
    for k in range(8):
        up2 = mm(fb2, hv[:, chunk(k)])
        up2 = up2[0:16] + up2[16:32]
        up_part = 2.0 * (f0 * dn_s[8:9, chunk(k)] + f1 * dn_s[9:10, chunk(k)] - up2)
        for t in range(wc // 128):
            put(tiles_down + k * (wc // 128) + t, up_part[:, t * 128 : t * 128 + 128])

    def half(which):
        return pl.ds(pl.multiple_of(8 * which, 8), 8)

    other = 1 - core
    swap = pltpu.make_async_remote_copy(
        src_ref=ab.at[:, half(other), :],
        dst_ref=core_in,
        send_sem=c_send,
        recv_sem=c_recv,
        device_id=(grp, 2 * q_me + other),
        device_id_type=MESH,
    )
    swap.start()

    swap.wait_recv()
    mine = half(core)
    core_in[...] = core_in[...] + ab[:, mine, :]
    plane_in[q_me] = core_in[q_me]
    fan_out(nq, plane_peer, lambda there: core_in.at[there], plane_in, q_me, p_sems)
    w_step4()

    row_id = iota((128, tok), 0)
    col_s[...] = jnp.transpose(jnp.where(row_id == 0, w0 + w1, jnp.where(row_id == 1, b, 0.0)))
    blf = jnp.concatenate([blt.astype(F32), jnp.zeros((112, tok), F32)], axis=0)
    bl_s[...] = jnp.transpose(blf).astype(BF16)

    def rows_dy(i, carry):
        rows = pl.ds(pl.multiple_of(i * 16, 16), 16)
        c = col_s[rows, :]
        second = jnp.where(i * 16 >= offsets[1], 1, 0)
        dn_row = dn_s[pl.ds(8 + second, 1), :]
        dyv[rows, :] = (c[:, 0:1] * dn_row - c[:, 1:2] * hv[rows, :].astype(F32)).astype(BF16)
        return carry

    lax.fori_loop(0, tok // 16, rows_dy, 0, unroll=2)

    fan_wait(nq, plane_in, p_sems)
    z_in[grp] = jnp.sum(plane_in[...], axis=0)
    fan_out(ng, z_peer, lambda there: z_in.at[grp], z_in, grp, z_sems)
    w_step5()

    fan_wait(nl, rub, v_sems)
    d_unit = 50.0 * jnp.sum(rub[...].astype(F32), axis=0)
    unit = unit_s[...]
    unit_s[...] = (d_unit - unit * pair_sum(jnp.sum(unit * d_unit, axis=1, keepdims=True))) / qnorm
    for k in range(8):
        query_out[:, chunk(k)] = unit_s[2 * k : 2 * k + 2, :]
    fan_wait(nq, ll, l_sems)
    loss_out[...] = jnp.sum(ll[...], axis=0)[0:1, 0:1] * (1.0 / passages)
    w_finish(4 * y_me + x_me + 1 - 2 * lax.rem(x_me, 2))
    tile_start(1)
    tile(0, 0)
    tile_start(2)
    tile(1, 0)

    fan_wait(ng, z_in, z_sems)
    total_s[q_me, mine, :] = jnp.sum(z_in[...], axis=0)

    def gather_piece(o, carry):
        there, device = plane_peer(o)
        pltpu.make_async_remote_copy(
            src_ref=total_s.at[q_me, mine, :],
            dst_ref=total_s.at[q_me, mine, :],
            send_sem=g_sems.at[0],
            recv_sem=g_sems.at[1],
            device_id=device,
            device_id_type=MESH,
        ).start()
        return carry

    lax.fori_loop(1, nq, gather_piece, 0)
    tile_start(3)
    tile(2, 0)
    tile_start(4)
    tile(3, 0)
    amount(total_s.at[0 : nq - 1, mine, :], g_sems).wait_recv()
    back = pltpu.make_async_remote_copy(
        src_ref=total_s.at[:, mine, :],
        dst_ref=total_s.at[:, mine, :],
        send_sem=s_send,
        recv_sem=s_recv,
        device_id=(grp, 2 * q_me + other),
        device_id_type=MESH,
    )
    back.start()

    def tiles(t, carry):
        tile_start(t + 1)
        return tile(t, carry)

    lax.fori_loop(4, 7, tiles, 0)
    tile(7, 0)

    back.wait_recv()
    for t in range(tiles_down):
        down_out[:, t * 128 : t * 128 + 128] = get(total_s, t)
    for t in range(tiles_up):
        up_out[:, t * 128 : t * 128 + 128] = get(total_s, tiles_down + t)
    fan_drain(nl, ub, u_sems)
    fan_drain(nq, eb, e_sems)
    fan_drain(nl, lx, x_sems)
    fan_drain(nq, dpb, d_sems)
    fan_drain(nq, ll, l_sems)
    fan_drain(nl, dub, v_sems)
    fan_drain(nq, core_in, p_sems)
    fan_drain(ng, z_in, z_sems)
    amount(total_s.at[0 : nq - 1, mine, :], g_sems).wait_send()
    swap.wait_send()
    back.wait_send()
    w_drain()


def finish(*refs):
    count = len(refs) // 2
    copies = []
    rows = refs[0].shape[0] // 8
    for i in range(8):
        part = pl.ds(i * rows, rows)
        copies.append(pltpu.make_async_copy(refs[0].at[part, :], refs[count].at[part, :], refs[-1].at[i]))
    for i in range(1, count):
        copies.append(pltpu.make_async_copy(refs[i], refs[count + i], refs[-1].at[7 + i]))
    for copy in copies:
        copy.start()
    for copy in copies:
        copy.wait()


def per_device(ng, nq, attn, hidden, weight, down, up, gain, queries, lengths, offsets, positives):
    tok, width = hidden.shape
    feat = attn.shape[1]
    wc = width // 8
    nl = 2 * ng
    piece = (feat + width) // nq
    vmem = pl.BlockSpec(memory_space=pltpu.VMEM)
    hbm = pl.BlockSpec(memory_space=pltpu.HBM)
    dma = pltpu.SemaphoreType.DMA
    outs = (
        jax.ShapeDtypeStruct((tok, feat), BF16),
        jax.ShapeDtypeStruct((2, width), F32),
        jax.ShapeDtypeStruct((16, feat), F32),
        jax.ShapeDtypeStruct((16, width), F32),
        jax.ShapeDtypeStruct((1, 1), F32),
    )
    results = pl.pallas_call(
        functools.partial(kernel, ng, nq),
        out_shape=outs,
        in_specs=[hbm] * 10,
        out_specs=(vmem,) * 5,
        scratch_shapes=[
            pltpu.VMEM((tok, width), BF16),
            pltpu.VMEM((tok, feat), BF16),
            pltpu.VMEM((2 * nq, 64, width), BF16),
            pltpu.VMEM((tok, width), BF16),
            pltpu.VMEM((16, feat), BF16),
            pltpu.VMEM((16, width), BF16),
            pltpu.VMEM((1, width), F32),
            pltpu.VMEM((2, width), BF16),
            pltpu.SMEM((2,), jnp.int32),
            pltpu.SMEM((2,), jnp.int32),
            pltpu.SMEM((2,), jnp.int32),
            pltpu.VMEM((nl, 16, wc + 128), BF16),
            pltpu.VMEM((nq, 16, wc), BF16),
            pltpu.VMEM((16, wc), F32),
            pltpu.VMEM((16, wc), F32),
            pltpu.VMEM((tok, 128), F32),
            pltpu.VMEM((tok, 128), F32),
            pltpu.VMEM((tok, 128), BF16),
            pltpu.VMEM((16, width), F32),
            pltpu.VMEM((nl, 8, 128), F32),
            pltpu.VMEM((nq, 8, 128), F32),
            pltpu.VMEM((nq, 16, wc), BF16),
            pltpu.VMEM((nq, 16, wc), BF16),
            pltpu.VMEM((nl, 16, wc), BF16),
            pltpu.VMEM((nl, 16, wc), BF16),
            pltpu.VMEM((nq, 16, piece), F32),
            pltpu.VMEM((nq, 8, piece), F32),
            pltpu.VMEM((nq, 8, piece), F32),
            pltpu.VMEM((ng, 8, piece), F32),
            pltpu.VMEM((nq, 16, piece), F32),
            dma((10,)),
            dma((2,)),
            dma((2,)),
            dma((2,)),
            dma((2,)),
            dma((2,)),
            dma((2,)),
            dma,
            dma,
            dma((2,)),
            dma((2,)),
            dma((2,)),
            dma,
            dma,
            dma((2,)),
            dma((2, 3, nq)),
            dma,
            dma((nq,)),
            dma,
            dma((2, nq)),
        ],
        compiler_params=pltpu.CompilerParams(
            collective_id=0, has_side_effects=True, vmem_limit_bytes=56 * 1024 * 1024
        ),
    )(hidden, attn, weight, down.T, up, gain.reshape(1, width), queries, lengths, offsets, positives)
    attention, query, down_sum, up_sum, loss = pl.pallas_call(
        finish,
        out_shape=outs,
        in_specs=[vmem] * 5,
        out_specs=(hbm,) * 5,
        scratch_shapes=[dma((12,))],
    )(*results)
    return attention, query, down_sum.T, up_sum, loss.reshape(())


def solution(mesh):
    ng = mesh.shape["grp"]
    nq = mesh.shape["dp"] // 2
    both = P(("grp", "dp"))
    rows = P(("grp", "dp"), None)
    return jax.shard_map(
        functools.partial(per_device, ng, nq),
        mesh=mesh,
        in_specs=(rows, rows, P("dp", None), P(), P(), P(), rows, both, both, both),
        out_specs=(rows, rows, P(), P(), P()),
        check_vma=False,
    )
```

time: 107 us -> 80.7 us (0.75)
  Pallas kernels: 99 us -> 79.9 us
  local copies, waits for them, and re-layouts: 5.19 us -> 0 us
  between operations: 2.37 us -> 0.64 us
    pallas_call x1, Pallas kernels: 99 us -> 76.1 us  [per_device(): pl.pallas_call(functools.partial(kernel, ng, nq), out_shape=outs, in_spec...]
    unnamed x10 -> x0, local copies, waits for them, and re-layouts: 5.19 us -> none
    pallas_call x0 -> x1, Pallas kernels: none -> 3.8 us  [per_device(): pl.pallas_call(finish, out_shape=outs, in_specs=[vmem] * 5, out_specs=(hb...]
where the time goes in v3:
time: 80.7 us; the launch traced here: 80.5 us
  Pallas kernels  79.9 us (99%)
    pallas_call x1, Pallas kernels, per_device(): pl.pallas_call(functools.partial(kernel, ng, nq), out_shape=outs, in_spec...  76.1 us
    pallas_call x1, Pallas kernels, per_device(): pl.pallas_call(finish, out_shape=outs, in_specs=[vmem] * 5, out_specs=(hb...  3.8 us

profile of v3, /device:TPU:1, one launch (start us, length us, event | category | flops | bytes accessed | tf_op | source)
XLA Modules:
  0.0 80.5 jit_solution(8449319166469421043)
XLA Ops:
  0.6 76.1 %shard_map.137 = (bf16[512,2048]{1,0:T(8,128)(2,1)}, f32[2,4096]{1,0:T(2,128)}, f32[16,2048]{1,0:T(8,128)}, f32[16,4096]{1,0:T(8,128)}, f32[1,1]{1,0:T(1,128)}) custom-call(bf16[512,4096]{1,0:T(8,128)(2,1)} %hidden.1, bf16[512,2048]{1,0:T(8,128)(2,1)} %attn.1, bf16[64,4096]{1,0:T(8,128)(2,1)} %weight.1, bf16[16,2048]{1,0:T(8,128)(2,1)} %bitcast.4, ...), custom_call_target="tpu_custom_call" | custom-call | tf_op jit(solution)/shard_map/pallas_call | solution.py:724
  76.7 3.8 %shard_map.138 = (bf16[512,2048]{1,0:T(8,128)(2,1)}, f32[2,4096]{1,0:T(2,128)}, f32[16,2048]{1,0:T(8,128)}, f32[16,4096]{1,0:T(8,128)}, f32[1,1]{1,0:T(1,128)}) custom-call(bf16[512,2048]{1,0:T(8,128)(2,1)} %get-tuple-element.15.refs_0_, f32[2,4096]{1,0:T(2,128)} %get-tuple-element.16.refs_1_, f32[16,2048]{1,0:T(8,128)} %get-tuple-element.17.refs_2_, ...), custom_call_target="tpu_custom_call" | custom-call | tf_op jit(solution)/shard_map/pallas_call | solution.py:785

commit v4 on v3

--- a/solution.py
+++ b/solution.py
@@ -54,6 +54,11 @@
     av,
     wv,
     dyv,
+    ov,
+    query_s,
+    down_s,
+    up_s,
+    loss_s,
     down_t,
     up,
     gain,
@@ -81,6 +86,7 @@
     z_in,
     total_s,
     local_sem,
+    out_sem,
     u_sems,
     e_sems,
     x_sems,
@@ -331,32 +337,40 @@
 
     def w_step3():
         for part in (0, 1):
-            w_far(part, 1, 0)
             w_wait(part, 2, 0)
             w_near(part, 1, 2)
+            w_far(part, 1, 0)
         for part in (0, 1):
             for o in (1, 3):
                 w_wait(part, o, 1)
                 w_wait(part, o, 3)
                 w_far(part, 1, o)
+        for oy, ox in ((1, 1), (1, 3), (3, 1), (3, 3)):
+            w_arrived(at(oy, ox))
 
     def w_step4():
+        for part in (0, 1):
+            w_wait(part, 0, 2)
+        for oy, ox in ((0, 2), (2, 0)):
+            w_arrived(at(oy, ox))
+
+    def w_step45():
         for part in (0, 1):
             w_wait(part, 2, 1)
             w_wait(part, 2, 3)
             w_far(part, 1, 2)
-        for part in (0, 1):
-            w_wait(part, 0, 2)
-        for oy, ox in ((0, 2), (2, 0), (1, 1), (1, 3), (3, 1), (3, 3)):
-            w_arrived(at(oy, ox))
 
     def w_step5():
         for part in (0, 1):
             w_wait(part, 1, 2)
             w_wait(part, 3, 2)
+        for oy, ox in ((1, 2), (3, 2), (2, 1), (2, 3)):
+            w_arrived(at(oy, ox))
+
+    def w_step6():
+        for part in (0, 1):
             w_wait(part, 2, 2)
-        for oy, ox in ((1, 2), (3, 2), (2, 1), (2, 3), (2, 2)):
-            w_arrived(at(oy, ox))
+        w_arrived(at(2, 2))
 
     def tile_at(t):
         def pick(values):
@@ -388,8 +402,19 @@
         columns = pl.ds(pl.multiple_of(256 * n, 256), 256)
         w_tile = wv[pl.ds(4 * n, 4)].reshape(256, width)
         out = mm(dyv[...], w_tile, NT) + mm(bl_s[:, 0:16], down_t[:, columns])
-        attn_out[:, columns] = out.astype(BF16)
+        ov[:, columns] = out.astype(BF16)
+        pltpu.make_async_copy(ov.at[:, columns], attn_out.at[:, columns], out_sem.at[t]).start()
         return carry
+
+    def tile_stored(t, carry):
+        columns = pl.ds(pl.multiple_of(256 * tile_at(t), 256), 256)
+        pltpu.make_async_copy(ov.at[:, columns], attn_out.at[:, columns], out_sem.at[t]).wait()
+        return carry
+
+    def store(source, target, i):
+        copy = pltpu.make_async_copy(source, target, local_sem.at[i])
+        copy.start()
+        return copy
 
     def w_drain():
         taken(wv.at[0:15, 0:32, :], w_send.at[0]).wait_send()
@@ -529,7 +554,9 @@
     rub[l_me] = dub[l_me]
     fan_out(nl, line_peer, lambda there: dub.at[there], rub, l_me, v_sems)
 
+    w_step4()
     fan_wait(nq, rb, d_sems)
+    w_step45()
     d_embed = 50.0 * jnp.sum(rb[...].astype(F32), axis=0)
     shared = pair_sum(jnp.sum(embed * d_embed, axis=1, keepdims=True))
     pool_s[...] = (d_embed - embed * shared) / pnorm / counts
@@ -597,7 +624,7 @@
     core_in[...] = core_in[...] + ab[:, mine, :]
     plane_in[q_me] = core_in[q_me]
     fan_out(nq, plane_peer, lambda there: core_in.at[there], plane_in, q_me, p_sems)
-    w_step4()
+    w_step5()
 
     row_id = iota((128, tok), 0)
     col_s[...] = jnp.transpose(jnp.where(row_id == 0, w0 + w1, jnp.where(row_id == 1, b, 0.0)))
@@ -617,16 +644,18 @@
     fan_wait(nq, plane_in, p_sems)
     z_in[grp] = jnp.sum(plane_in[...], axis=0)
     fan_out(ng, z_peer, lambda there: z_in.at[grp], z_in, grp, z_sems)
-    w_step5()
+    w_step6()
 
     fan_wait(nl, rub, v_sems)
     d_unit = 50.0 * jnp.sum(rub[...].astype(F32), axis=0)
     unit = unit_s[...]
     unit_s[...] = (d_unit - unit * pair_sum(jnp.sum(unit * d_unit, axis=1, keepdims=True))) / qnorm
     for k in range(8):
-        query_out[:, chunk(k)] = unit_s[2 * k : 2 * k + 2, :]
+        query_s[:, chunk(k)] = unit_s[2 * k : 2 * k + 2, :]
+    stored = [store(query_s, query_out, 10)]
     fan_wait(nq, ll, l_sems)
-    loss_out[...] = jnp.sum(ll[...], axis=0)[0:1, 0:1] * (1.0 / passages)
+    loss_s[...] = jnp.sum(ll[...], axis=0)[0:1, 0:1] * (1.0 / passages)
+    stored.append(store(loss_s, loss_out, 11))
     w_finish(4 * y_me + x_me + 1 - 2 * lax.rem(x_me, 2))
     tile_start(1)
     tile(0, 0)
@@ -673,9 +702,11 @@
 
     back.wait_recv()
     for t in range(tiles_down):
-        down_out[:, t * 128 : t * 128 + 128] = get(total_s, t)
+        down_s[:, t * 128 : t * 128 + 128] = get(total_s, t)
     for t in range(tiles_up):
-        up_out[:, t * 128 : t * 128 + 128] = get(total_s, tiles_down + t)
+        up_s[:, t * 128 : t * 128 + 128] = get(total_s, tiles_down + t)
+    stored.append(store(down_s, down_out, 12))
+    stored.append(store(up_s, up_out, 13))
     fan_drain(nl, ub, u_sems)
     fan_drain(nq, eb, e_sems)
     fan_drain(nl, lx, x_sems)
@@ -688,20 +719,30 @@
     swap.wait_send()
     back.wait_send()
     w_drain()
+    lax.fori_loop(0, 8, tile_stored, 0)
+    for copy in stored:
+        copy.wait()
 
 
 def finish(*refs):
-    count = len(refs) // 2
-    copies = []
-    rows = refs[0].shape[0] // 8
-    for i in range(8):
-        part = pl.ds(i * rows, rows)
-        copies.append(pltpu.make_async_copy(refs[0].at[part, :], refs[count].at[part, :], refs[-1].at[i]))
-    for i in range(1, count):
-        copies.append(pltpu.make_async_copy(refs[i], refs[count + i], refs[-1].at[7 + i]))
-    for copy in copies:
+    sources, targets, stages, sems = refs[0:5], refs[5:10], refs[10:15], refs[15]
+    rows = sources[0].shape[0] // 8
+    pieces = [(0, pl.ds(i * rows, rows)) for i in range(8)]
+    pieces += [(k, slice(None)) for k in range(1, 5)]
+    arriving = [
+        pltpu.make_async_copy(sources[k].at[part, :], stages[k].at[part, :], sems.at[0, i])
+        for i, (k, part) in enumerate(pieces)
+    ]
+    leaving = [
+        pltpu.make_async_copy(stages[k].at[part, :], targets[k].at[part, :], sems.at[1, i])
+        for i, (k, part) in enumerate(pieces)
+    ]
+    for copy in arriving:
         copy.start()
-    for copy in copies:
+    for first, then in zip(arriving, leaving):
+        first.wait()
+        then.start()
+    for copy in leaving:
         copy.wait()
 
 
@@ -711,7 +752,6 @@
     wc = width // 8
     nl = 2 * ng
     piece = (feat + width) // nq
-    vmem = pl.BlockSpec(memory_space=pltpu.VMEM)
     hbm = pl.BlockSpec(memory_space=pltpu.HBM)
     dma = pltpu.SemaphoreType.DMA
     outs = (
@@ -721,16 +761,18 @@
         jax.ShapeDtypeStruct((16, width), F32),
         jax.ShapeDtypeStruct((1, 1), F32),
     )
+    stages = [pltpu.VMEM(out.shape, out.dtype) for out in outs]
     results = pl.pallas_call(
         functools.partial(kernel, ng, nq),
         out_shape=outs,
         in_specs=[hbm] * 10,
-        out_specs=(vmem,) * 5,
+        out_specs=(hbm,) * 5,
         scratch_shapes=[
             pltpu.VMEM((tok, width), BF16),
             pltpu.VMEM((tok, feat), BF16),
             pltpu.VMEM((2 * nq, 64, width), BF16),
             pltpu.VMEM((tok, width), BF16),
+            *stages,
             pltpu.VMEM((16, feat), BF16),
             pltpu.VMEM((16, width), BF16),
             pltpu.VMEM((1, width), F32),
@@ -757,7 +799,8 @@
             pltpu.VMEM((nq, 8, piece), F32),
             pltpu.VMEM((ng, 8, piece), F32),
             pltpu.VMEM((nq, 16, piece), F32),
-            dma((10,)),
+            dma((14,)),
+            dma((8,)),
             dma((2,)),
             dma((2,)),
             dma((2,)),
@@ -785,9 +828,9 @@
     attention, query, down_sum, up_sum, loss = pl.pallas_call(
         finish,
         out_shape=outs,
-        in_specs=[vmem] * 5,
+        in_specs=[hbm] * 5,
         out_specs=(hbm,) * 5,
-        scratch_shapes=[dma((12,))],
+        scratch_shapes=[*stages, dma((2, 12))],
     )(*results)
     return attention, query, down_sum.T, up_sum, loss.reshape(())
 

time: 80.7 us -> 79 us (0.979)
  Pallas kernels: 79.9 us -> 78.2 us
    pallas_call x1, Pallas kernels: 76.1 us -> 75 us  [per_device(): pl.pallas_call(functools.partial(kernel, ng, nq), out_shape=outs, in_spec...]
where the time goes in v4:
time: 79 us; the launch traced here: 78.8 us
  Pallas kernels  78.2 us (99%)
    pallas_call x1, Pallas kernels, per_device(): pl.pallas_call(functools.partial(kernel, ng, nq), out_shape=outs, in_spec...  75 us
    pallas_call x1, Pallas kernels, per_device(): pl.pallas_call(finish, out_shape=outs, in_specs=[hbm] * 5, out_specs=(hbm...  3.22 us

profile of v4, /device:TPU:1, one launch (start us, length us, event | category | flops | bytes accessed | tf_op | source)
XLA Modules:
  0.0 78.8 jit_solution(11190503487754240102)
XLA Ops:
  0.6 75.0 %shard_map.137 = (bf16[512,2048]{1,0:T(8,128)(2,1)}, f32[2,4096]{1,0:T(2,128)}, f32[16,2048]{1,0:T(8,128)}, f32[16,4096]{1,0:T(8,128)}, f32[1,1]{1,0:T(1,128)}) custom-call(bf16[512,4096]{1,0:T(8,128)(2,1)} %hidden.1, bf16[512,2048]{1,0:T(8,128)(2,1)} %attn.1, bf16[64,4096]{1,0:T(8,128)(2,1)} %weight.1, bf16[16,2048]{1,0:T(8,128)(2,1)} %bitcast.4, ...), custom_call_target="tpu_custom_call" | custom-call | tf_op jit(solution)/shard_map/pallas_call | solution.py:765
  75.6 3.2 %shard_map.138 = (bf16[512,2048]{1,0:T(8,128)(2,1)}, f32[2,4096]{1,0:T(2,128)}, f32[16,2048]{1,0:T(8,128)}, f32[16,4096]{1,0:T(8,128)}, f32[1,1]{1,0:T(1,128)}) custom-call(bf16[512,2048]{1,0:T(8,128)(2,1)} %get-tuple-element.15.refs_0_, f32[2,4096]{1,0:T(2,128)} %get-tuple-element.16.refs_1_, f32[16,2048]{1,0:T(8,128)} %get-tuple-element.17.refs_2_, ...), custom_call_target="tpu_custom_call" | custom-call | tf_op jit(solution)/shard_map/pallas_call | solution.py:828
